TPU v7x, 32 devices: a whole 2x2x4 slice. The times are simulated.
32 devices in a mesh: row: 8 (over y, x, core), col: 4 (over z).
Axes of the slice: x: 2, y: 2, z: 4, core: 2. Of those that a mesh axis runs over, the one named last changes fastest.
Arguments:
- row_frames: float32 [3, 1024, 256], P(None, ('row', 'col')), may hold values from -40 to 40, as said below
- col_frames: float32 [3, 1024, 256], P(None, ('col', 'row')), may hold values from -40 to 40, as said below
- vectors: float32 [64, 1024], P(None, ('col', 'row')), may hold values from -6 to 6
Outputs:
- embedding_product: float32 [64, 1024], P(None, ('row', 'col'))
Inputs may be any that keep to these rules, and one draw needn't show every extreme that they name: `row_frames`: frames of one chain of 256 atoms, each rigidly rotated and moved and perturbed by its own amount. `col_frames`: frames of one chain of 256 atoms, each rigidly rotated and moved and perturbed by its own amount.
All inputs are finite; a program needn't handle non-finite values.
Results may differ from a plain program's by a relative error of at most 0.00017.
Values sent between devices are 32-bit elements; how exact they have to be, the bound alone decides.
No kernel may reach another device: no remote copies, remote signals or barrier semaphores. Data moves between devices by JAX's collectives and lax.ppermute only.
A program may use at most 64 MiB of HBM per device.

v0:
```python
import functools

import jax
import jax.numpy as jnp
from jax import lax
from jax.experimental import pallas as pl
from jax.experimental.pallas import tpu as pltpu
from jax.sharding import PartitionSpec as P

NEWTON = 8
BAND = 2.0
LANES = 128
VM = pl.BlockSpec(memory_space=pltpu.VMEM)
NT = (((1,), (1,)), ((), ()))


def centre(frames):
    return frames - jnp.mean(frames, axis=-1, keepdims=True)


def split(x):
    high = x.astype(jnp.bfloat16)
    low = (x - high.astype(jnp.float32)).astype(jnp.bfloat16)
    return high, low


def copy_kernel(in_ref, out_ref):
    out_ref[...] = in_ref[...]


def join_kernel(first_ref, second_ref, out_ref):
    count = second_ref.shape[0]
    out_ref[0:count] = first_ref[...]
    out_ref[count:] = second_ref[...]


def after_far_kernel(far_ref, vec_ref, got_ref, far_out, vec_out):
    far_out[...] = far_ref[...]
    join_kernel(vec_ref, got_ref, vec_out)


def columns_kernel(n_blocks, *refs):
    for at in range(n_blocks):
        refs[-1][at] = refs[at][...]


def inverse(x):
    guess = pl.reciprocal(x, approx=True)
    return guess * (2.0 - x * guess)


def eigen_tile(m, half_norm, atoms):
    s00, s01, s02, s10, s11, s12, s20, s21, s22 = m
    coef_two = -2.0 * (
        s00 * s00 + s01 * s01 + s02 * s02 + s10 * s10 + s11 * s11 + s12 * s12 + s20 * s20 + s21 * s21 + s22 * s22
    )
    coef_one = 8.0 * (s00 * s12 * s21 + s11 * s20 * s02 + s22 * s01 * s10) - 8.0 * (
        s00 * s11 * s22 + s12 * s20 * s01 + s21 * s10 * s02
    )
    k00 = s00 + s11 + s22
    k11 = s00 - s11 - s22
    k22 = s11 - s00 - s22
    k33 = s22 - s00 - s11
    k01 = s12 - s21
    k02 = s20 - s02
    k03 = s01 - s10
    k12 = s01 + s10
    k13 = s20 + s02
    k23 = s12 + s21
    top0 = k00 * k11 - k01 * k01
    top1 = k00 * k12 - k01 * k02
    top2 = k00 * k13 - k01 * k03
    top3 = k01 * k12 - k11 * k02
    top4 = k01 * k13 - k11 * k03
    top5 = k02 * k13 - k12 * k03
    low0 = k02 * k13 - k03 * k12
    low1 = k02 * k23 - k03 * k22
    low2 = k02 * k33 - k03 * k23
    low3 = k12 * k23 - k13 * k22
    low4 = k12 * k33 - k13 * k23
    low5 = k22 * k33 - k23 * k23
    coef_zero = top0 * low5 - top1 * low4 + top2 * low3 + top3 * low2 - top4 * low1 + top5 * low0
    eigen = half_norm
    twice = coef_two + coef_two
    for _ in range(NEWTON):
        eigen_sq = eigen * eigen
        value = (eigen_sq + coef_two) * eigen_sq + coef_one * eigen + coef_zero
        slope = (4.0 * eigen_sq + twice) * eigen + coef_one
        eigen = eigen - value * inverse(slope)
    squared = jnp.maximum(2.0 * (half_norm - eigen) / atoms, 0.0)
    return jnp.exp(-squared / BAND)


def column_side(blocks_ref, vecs_ref):
    count, _, frames, atoms = blocks_ref.shape
    nv = vecs_ref.shape[2]
    cols = [
        centre(jnp.concatenate([blocks_ref[at, comp] for at in range(count)], axis=0)) for comp in range(3)
    ]
    col_square = cols[0] * cols[0] + cols[1] * cols[1] + cols[2] * cols[2]
    norm = lax.dot_general(
        jnp.ones((8, atoms), jnp.float32), col_square, NT,
        precision=lax.Precision.HIGHEST, preferred_element_type=jnp.float32,
    )[0:1, :]
    high, low = split(jnp.concatenate(cols, axis=0))
    side = jnp.concatenate([high, high, low], axis=1)
    ones = jnp.where(lax.broadcasted_iota(jnp.int32, (count * frames, LANES - nv), 1) == 0, 1.0, 0.0)
    vecs = jnp.concatenate([vecs_ref[at] for at in range(count)], axis=0)
    high, low = split(jnp.concatenate([vecs, ones], axis=1))
    return side, norm, jnp.concatenate([high, high, low], axis=0)


def multiply(row_side, row_norm, side, norm, vec, atoms, moment, tile):
    count = row_norm.shape[0]
    count_cols = norm.shape[1]
    moment[...] = lax.dot_general(row_side, side, NT, preferred_element_type=jnp.float32)
    for at in range(0, count, 8):
        m = [
            moment[a * count + at:a * count + at + 8, b * count_cols:(b + 1) * count_cols]
            for a in range(3) for b in range(3)
        ]
        half_norm = 0.5 * (row_norm[at:at + 8, 0:1] + norm)
        tile[at:at + 8, :] = eigen_tile(m, half_norm, atoms)
    high, low = split(tile[...])
    return jnp.dot(jnp.concatenate([high, low, high], axis=1), vec, preferred_element_type=jnp.float32)


def first_kernel(n_mine, *refs):
    slots, blocks_ref, vecs_ref = refs[:n_mine], refs[n_mine], refs[n_mine + 1]
    sum_ref, side_ref, norm_ref, moment, tile = refs[n_mine + 2:]
    _, frames, atoms = slots[0].shape
    groups, count, _ = sum_ref.shape
    side, norm, vec = column_side(blocks_ref, vecs_ref)
    for group in range(groups):
        own = slots[group * count // frames:(group + 1) * count // frames]
        rows = [centre(jnp.concatenate([ref[comp] for ref in own], axis=0)) for comp in range(3)]
        square = jnp.sum(rows[0] * rows[0] + rows[1] * rows[1] + rows[2] * rows[2], axis=1, keepdims=True)
        row_norm = jnp.broadcast_to(square, (count, LANES))
        high, low = split(jnp.concatenate(rows, axis=0))
        row_side = jnp.concatenate([high, low, high], axis=1)
        side_ref[group] = row_side
        norm_ref[group] = row_norm
        sum_ref[group] = multiply(row_side, row_norm, side, norm, vec, atoms, moment, tile)


def second_kernel(frames, sum_ref, side_ref, norm_ref, blocks_ref, vecs_ref, *refs):
    moment, tile = refs[-2:]
    atoms = blocks_ref.shape[-1]
    groups, count, _ = sum_ref.shape
    side, norm, vec = column_side(blocks_ref, vecs_ref)
    for group in range(groups):
        total = sum_ref[group] + multiply(side_ref[group], norm_ref[group], side, norm, vec, atoms, moment, tile)
        for at in range(count // frames):
            refs[group * count // frames + at][...] = total[at * frames:(at + 1) * frames, :]


def finish_kernel(nv, *refs):
    total = refs[0][...]
    for ref in refs[1:-1]:
        total = total + ref[...]
    refs[-1][...] = total[:, 0:nv] / total[:, nv:nv + 1]


def exchange(x, axis, mask, count):
    return lax.ppermute(x, axis, [(at, at ^ mask) for at in range(count)])


def call(kernel, outs, ins, name, scratch=(), megabytes=8, flops=0):
    out_shape = [jax.ShapeDtypeStruct(*out) for out in outs]
    moved = sum(x.size * 4 for x in ins)
    return pl.pallas_call(
        kernel,
        out_shape=out_shape,
        in_specs=[VM] * len(ins),
        out_specs=[VM] * len(outs),
        scratch_shapes=list(scratch),
        compiler_params=pltpu.CompilerParams(vmem_limit_bytes=megabytes * 1024 * 1024),
        cost_estimate=pl.CostEstimate(flops=flops, bytes_accessed=moved, transcendentals=0),
        name=name,
    )(*ins)


def per_device(n_row, n_col, row_frames, col_frames, vectors):
    comps, frames, atoms = row_frames.shape
    nv = vectors.shape[0]
    f32, bf16 = jnp.float32, jnp.bfloat16
    row_masks = [n_col >> at for at in range(1, n_col.bit_length())]
    col_masks = [1 << at for at in range(1, n_row.bit_length() - 1)]

    vecs = vectors.T[None]
    got_vecs = exchange(vecs, "row", col_masks[0], n_row)
    (vecs,) = call(copy_kernel, [((1, frames, nv), f32)], [vecs], "vectors", flops=1 << 30)
    order = [0]
    rows = {0: row_frames}
    for mask in row_masks:
        for slot in list(order):
            got = exchange(rows[slot], "col", mask, n_col)
            if not slot and mask == row_masks[0]:
                got, vecs = call(
                    after_far_kernel, [(got.shape, f32), ((2, frames, nv), f32)], [got, vecs, got_vecs], "after_far"
                )
            rows[slot ^ mask] = got
            order.append(slot ^ mask)
    col_order = [0]
    for mask in col_masks:
        col_order = col_order + [slot ^ mask for slot in col_order]
    cols = [col_frames] + [exchange(col_frames, "row", mask, n_row) for mask in col_order[1:]]
    for mask in col_masks[1:]:
        got = exchange(vecs, "row", mask, n_row)
        (vecs,) = call(join_kernel, [((2 * vecs.shape[0], frames, nv), f32)], [vecs, got], "vectors")
    (blocks,) = call(
        functools.partial(columns_kernel, len(cols)), [((len(cols), *col_frames.shape), f32)],
        [*cols, rows[row_masks[0]], rows[row_masks[1]]], "columns", flops=10 << 30,
    )
    other = exchange(blocks, "row", 1, n_row)
    other_vecs = exchange(vecs, "row", 1, n_row)

    half_cols = n_row // 2 * frames
    count = min(n_col, max(1, LANES // frames)) * frames
    groups = n_col * frames // count
    scratch = [pltpu.VMEM((3 * count, 3 * half_cols), f32), pltpu.VMEM((count, half_cols), f32)]
    work = 2 * 3 * n_col * frames * 3 * half_cols * 3 * atoms
    sums, side, norm = call(
        functools.partial(first_kernel, n_col),
        [((groups, count, LANES), f32), ((groups, 3 * count, 3 * atoms), bf16), ((groups, count, LANES), f32)],
        [*[rows[slot] for slot in order], blocks, vecs], "first_tile", scratch, 32, work << 8,
    )
    parts = call(
        functools.partial(second_kernel, frames), [((frames, LANES), f32)] * n_col,
        [sums, side, norm, other, other_vecs], "second_tile", scratch, 32, work,
    )
    shares = [parts[0]] + [
        exchange(parts[order.index(mask)], "col", mask, n_col) for mask in range(n_col - 1, 0, -1)
    ]
    (result,) = call(functools.partial(finish_kernel, nv), [((frames, nv), f32)], shares, "sum_divide")
    return result.T


def solution(mesh):
    return jax.shard_map(
        functools.partial(per_device, mesh.shape["row"], mesh.shape["col"]),
        mesh=mesh,
        in_specs=(
            P(None, ("row", "col"), None),
            P(None, ("col", "row"), None),
            P(None, ("col", "row")),
        ),
        out_specs=P(None, ("row", "col")),
        check_vma=False,
    )
```

profile of v0, /device:TPU:0, one launch (start us, length us, event | category | flops | bytes accessed | tf_op | source)
XLA Modules:
  0.0 28.3 jit_solution(9715905940703003985)
XLA Ops:
  0.0 2.9 %collective-permute-start.1 = (f32[1,32,64]{2,1,0:T(8,128)}, f32[1,32,64]{2,1,0:T(8,128)S(1)}, u32[]{:S(2)}, u32[]{:S(2)}) collective-permute-start(f32[1,32,64]{2,1,0:T(8,128)} %bitcast.4), channel_id=1, source_target_pairs={{0,8},{4,12},{8,0},{12,4},{16,24},{20,28},{24,16},{28,20},{1,9},{5... | collective-permute-start | bytes 24584 | tf_op jit(solution)/shard_map/ppermute | solution.py:165
  2.9 2.6 %collective-permute-start = (f32[3,32,256]{2,1,0:T(8,128)}, f32[3,32,256]{2,1,0:T(8,128)S(1)}, u32[]{:S(2)}, u32[]{:S(2)}) collective-permute-start(f32[3,32,256]{2,1,0:T(8,128)} %refs_0_.3), channel_id=1, source_target_pairs={{0,2},{1,3},{2,0},{3,1},{4,6},{5,7},{6,4},{7,5},{8,10},{9,11},{10,... | collective-permute-start | bytes 294920 | tf_op jit(solution)/shard_map/ppermute | solution.py:165
  5.5 1.6 %collective-permute-start.2 = (f32[3,32,256]{2,1,0:T(8,128)}, f32[3,32,256]{2,1,0:T(8,128)S(1)}, u32[]{:S(2)}, u32[]{:S(2)}) collective-permute-start(f32[3,32,256]{2,1,0:T(8,128)} %refs_0_.3), channel_id=1, source_target_pairs={{0,1},{1,0},{2,3},{3,2},{4,5},{5,4},{6,7},{7,6},{8,9},{9,8},{10,11... | collective-permute-start | bytes 294920 | tf_op jit(solution)/shard_map/ppermute | solution.py:165
  7.1 1.5 %collective-permute-start.5 = (f32[3,32,256]{2,1,0:T(8,128)}, f32[3,32,256]{2,1,0:T(8,128)S(1)}, u32[]{:S(2)}, u32[]{:S(2)}) collective-permute-start(f32[3,32,256]{2,1,0:T(8,128)} %refs_0_.2), channel_id=1, source_target_pairs={{0,16},{4,20},{8,24},{12,28},{16,0},{20,4},{24,8},{28,12},{1,17},{... | collective-permute-start | bytes 294920 | tf_op jit(solution)/shard_map/ppermute | solution.py:165
  8.6 0.5 %collective-permute-start.4 = (f32[3,32,256]{2,1,0:T(8,128)}, f32[3,32,256]{2,1,0:T(8,128)S(1)}, u32[]{:S(2)}, u32[]{:S(2)}) collective-permute-start(f32[3,32,256]{2,1,0:T(8,128)} %refs_0_.2), channel_id=1, source_target_pairs={{0,8},{4,12},{8,0},{12,4},{16,24},{20,28},{24,16},{28,20},{1,9},{5... | collective-permute-start | bytes 294920 | tf_op jit(solution)/shard_map/ppermute | solution.py:165
  9.2 0.0 collective-permute-done.1.got_ref
  9.2 1.4 %collective-permute-start.6 = (f32[3,32,256]{2,1,0:T(8,128)}, f32[3,32,256]{2,1,0:T(8,128)S(1)}, u32[]{:S(2)}, u32[]{:S(2)}) collective-permute-start(f32[3,32,256]{2,1,0:T(8,128)} %refs_0_.2), channel_id=1, source_target_pairs={{0,24},{4,28},{8,16},{12,20},{16,8},{20,12},{24,0},{28,4},{1,25},{... | collective-permute-start | bytes 294920 | tf_op jit(solution)/shard_map/ppermute | solution.py:165
  10.6 0.7 %copy-done.2 = f32[64,32]{0,1:T(8,128)S(1)} copy-done((f32[64,32]{0,1:T(8,128)S(1)}, f32[64,32]{0,1:T(8,128)}, u32[]{:S(2)}) %copy-start.2) | copy-done | bytes 8216
  11.3 0.0 collective-permute-done.far_ref
  11.3 1.6 %collective-permute-start.7 = (f32[2,32,64]{2,1,0:T(8,128)S(1)}, f32[2,32,64]{2,1,0:T(8,128)S(1)}, u32[]{:S(2)}, u32[]{:S(2)}) collective-permute-start(f32[2,32,64]{2,1,0:T(8,128)S(1)} %get-tuple-element.15.first_ref), channel_id=1, source_target_pairs={{0,16},{4,20},{8,24},{12,28},{16,0},{20,4},{24,8},{28,12},{1,17},{... | collective-permute-start | bytes 49160 | tf_op jit(solution)/shard_map/ppermute | solution.py:165
  12.9 0.0 collective-permute-done.2.refs_5_.refs_2_
  12.9 0.5 %collective-permute-start.3 = (f32[3,32,256]{2,1,0:T(8,128)S(1)}, f32[3,32,256]{2,1,0:T(8,128)S(1)}, u32[]{:S(2)}, u32[]{:S(2)}) collective-permute-start(f32[3,32,256]{2,1,0:T(8,128)S(1)} %get-tuple-element.14.refs_4_.refs_1_), channel_id=1, source_target_pairs={{0,1},{1,0},{2,3},{3,2},{4,5},{5,4},{6,7},{7,6},{8,9},{9,8},{10,11... | collective-permute-start | bytes 294920 | tf_op jit(solution)/shard_map/ppermute | solution.py:165
  13.4 0.0 collective-permute-done.5.refs_2_
  13.4 0.1 collective-permute-done.4.refs_1_
  13.5 1.4 %collective-permute-done.6.refs_3_ = f32[3,32,256]{2,1,0:T(8,128)S(1)} collective-permute-done((f32[3,32,256]{2,1,0:T(8,128)}, f32[3,32,256]{2,1,0:T(8,128)S(1)}, u32[]{:S(2)}, u32[]{:S(2)}) %collective-permute-start.6) | collective-permute-done | bytes 98336 | tf_op jit(solution)/shard_map/ppermute | solution.py:165
  14.9 0.0 copy-done
  14.9 0.0 copy-start.1
  14.9 0.1 collective-permute-start.8
  15.0 0.3 %collective-permute-done.7.second_ref = f32[2,32,64]{2,1,0:T(8,128)S(1)} collective-permute-done((f32[2,32,64]{2,1,0:T(8,128)S(1)}, f32[2,32,64]{2,1,0:T(8,128)S(1)}, u32[]{:S(2)}, u32[]{:S(2)}) %collective-permute-start.7) | collective-permute-done | bytes 16416 | tf_op jit(solution)/shard_map/ppermute | solution.py:165
  15.3 0.3 collective-permute-start.9
  15.6 2.0 %collective-permute-done.3.refs_3_ = f32[3,32,256]{2,1,0:T(8,128)S(1)} collective-permute-done((f32[3,32,256]{2,1,0:T(8,128)S(1)}, f32[3,32,256]{2,1,0:T(8,128)S(1)}, u32[]{:S(2)}, u32[]{:S(2)}) %collective-permute-start.3) | collective-permute-done | bytes 98336 | tf_op jit(solution)/shard_map/ppermute | solution.py:165
  17.6 1.4 %first_tile.1 = (f32[1,128,128]{2,1,0:T(8,128)S(1)}, bf16[1,384,768]{2,1,0:T(8,128)(2,1)S(1)}, f32[1,128,128]{2,1,0:T(8,128)S(1)}) custom-call(f32[3,32,256]{2,1,0:T(8,128)S(1)} %copy-done.1, f32[3,32,256]{2,1,0:T(8,128)S(1)} %get-tuple-element.14.refs_4_.refs_1_, f32[3,32,256]{2,1,0:T(8,128)S(1)} %collective-permute-done.2.refs_5_.refs_2_, ...), custom_call_target="tpu_custom_call" | custom-call | flops 57982058496 | bytes 819200 | tf_op jit(solution)/shard_map/first_tile/pallas_call | solution.py:171
  18.9 0.0 collective-permute-done.9.vecs_ref
  18.9 0.0 collective-permute-done.8.blocks_ref
  18.9 1.3 %second_tile.1 = (f32[32,128]{1,0:T(8,128)S(1)}, f32[32,128]{1,0:T(8,128)S(1)}, f32[32,128]{1,0:T(8,128)S(1)}, f32[32,128]{1,0:T(8,128)S(1)}) custom-call(f32[1,128,128]{2,1,0:T(8,128)S(1)} %get-tuple-element.16.sum_ref, bf16[1,384,768]{2,1,0:T(8,128)(2,1)S(1)} %get-tuple-element.17.side_ref, f32[1,128,128]{2,1,0:T(8,128)S(1)} %get-tuple-element.18.norm_ref, ...), custom_call_target="tpu_custom_call" | custom-call | flops 226492416 | bytes 1736704 | tf_op jit(solution)/shard_map/second_tile/pallas_call | solution.py:171
  20.3 2.6 %collective-permute-start.10 = (f32[32,128]{1,0:T(8,128)S(1)}, f32[32,128]{1,0:T(8,128)S(1)}, u32[]{:S(2)}, u32[]{:S(2)}) collective-permute-start(f32[32,128]{1,0:T(8,128)S(1)} %get-tuple-element.20), channel_id=1, source_target_pairs={{0,3},{1,2},{2,1},{3,0},{4,7},{5,6},{6,5},{7,4},{8,11},{9,10},{10,... | collective-permute-start | bytes 49160 | tf_op jit(solution)/shard_map/ppermute | solution.py:165
  22.9 0.0 collective-permute-start.11
  22.9 1.8 %collective-permute-start.12 = (f32[32,128]{1,0:T(8,128)S(1)}, f32[32,128]{1,0:T(8,128)S(1)}, u32[]{:S(2)}, u32[]{:S(2)}) collective-permute-start(f32[32,128]{1,0:T(8,128)S(1)} %get-tuple-element.22), channel_id=1, source_target_pairs={{0,1},{1,0},{2,3},{3,2},{4,5},{5,4},{6,7},{7,6},{8,9},{9,8},{10,11... | collective-permute-start | bytes 49160 | tf_op jit(solution)/shard_map/ppermute | solution.py:165
  24.7 1.2 %collective-permute-done.10.refs_1_ = f32[32,128]{1,0:T(8,128)S(1)} collective-permute-done((f32[32,128]{1,0:T(8,128)S(1)}, f32[32,128]{1,0:T(8,128)S(1)}, u32[]{:S(2)}, u32[]{:S(2)}) %collective-permute-start.10) | collective-permute-done | bytes 16416 | tf_op jit(solution)/shard_map/ppermute | solution.py:165
  26.0 1.6 %collective-permute-done.11.refs_2_ = f32[32,128]{1,0:T(8,128)S(1)} collective-permute-done((f32[32,128]{1,0:T(8,128)S(1)}, f32[32,128]{1,0:T(8,128)S(1)}, u32[]{:S(2)}, u32[]{:S(2)}) %collective-permute-start.11) | collective-permute-done | bytes 16416 | tf_op jit(solution)/shard_map/ppermute | solution.py:165
  27.6 0.0 collective-permute-done.12.refs_3_
  27.6 0.7 %sum_divide.1 = f32[32,64]{1,0:T(8,128)} custom-call(f32[32,128]{1,0:T(8,128)S(1)} %get-tuple-element.19.refs_0_, f32[32,128]{1,0:T(8,128)S(1)} %collective-permute-done.10.refs_1_, f32[32,128]{1,0:T(8,128)S(1)} %collective-permute-done.11.refs_2_, f32[32,128]{1,0:T(8,128)S(1)} %collective-permute-done.12.refs_3_), custom_call_target="tpu_custom_call" | custom-call | bytes 65536 | tf_op jit(solution)/shard_map/sum_divide/pallas_call | solution.py:171
  (7 shorter events, 0.1 us)
Async XLA Ops:
  0.0 9.2 %collective-permute-start.1 = (f32[1,32,64]{2,1,0:T(8,128)}, f32[1,32,64]{2,1,0:T(8,128)S(1)}, u32[]{:S(2)}, u32[]{:S(2)}) collective-permute-start(f32[1,32,64]{2,1,0:T(8,128)} %bitcast.4), channel_id=1, source_target_pairs={{0,8},{4,12},{8,0},{12,4},{16,24},{20,28},{24,16},{28,20},{1,9},{5... | collective-permute-start | bytes 24584 | tf_op jit(solution)/shard_map/ppermute | solution.py:165
  2.9 8.4 %collective-permute-start = (f32[3,32,256]{2,1,0:T(8,128)}, f32[3,32,256]{2,1,0:T(8,128)S(1)}, u32[]{:S(2)}, u32[]{:S(2)}) collective-permute-start(f32[3,32,256]{2,1,0:T(8,128)} %refs_0_.3), channel_id=1, source_target_pairs={{0,2},{1,3},{2,0},{3,1},{4,6},{5,7},{6,4},{7,5},{8,10},{9,11},{10,... | collective-permute-start | bytes 294920 | tf_op jit(solution)/shard_map/ppermute | solution.py:165
  5.5 7.4 %collective-permute-start.2 = (f32[3,32,256]{2,1,0:T(8,128)}, f32[3,32,256]{2,1,0:T(8,128)S(1)}, u32[]{:S(2)}, u32[]{:S(2)}) collective-permute-start(f32[3,32,256]{2,1,0:T(8,128)} %refs_0_.3), channel_id=1, source_target_pairs={{0,1},{1,0},{2,3},{3,2},{4,5},{5,4},{6,7},{7,6},{8,9},{9,8},{10,11... | collective-permute-start | bytes 294920 | tf_op jit(solution)/shard_map/ppermute | solution.py:165
  7.1 6.3 %collective-permute-start.5 = (f32[3,32,256]{2,1,0:T(8,128)}, f32[3,32,256]{2,1,0:T(8,128)S(1)}, u32[]{:S(2)}, u32[]{:S(2)}) collective-permute-start(f32[3,32,256]{2,1,0:T(8,128)} %refs_0_.2), channel_id=1, source_target_pairs={{0,16},{4,20},{8,24},{12,28},{16,0},{20,4},{24,8},{28,12},{1,17},{... | collective-permute-start | bytes 294920 | tf_op jit(solution)/shard_map/ppermute | solution.py:165
  8.6 4.8 %collective-permute-start.4 = (f32[3,32,256]{2,1,0:T(8,128)}, f32[3,32,256]{2,1,0:T(8,128)S(1)}, u32[]{:S(2)}, u32[]{:S(2)}) collective-permute-start(f32[3,32,256]{2,1,0:T(8,128)} %refs_0_.2), channel_id=1, source_target_pairs={{0,8},{4,12},{8,0},{12,4},{16,24},{20,28},{24,16},{28,20},{1,9},{5... | collective-permute-start | bytes 294920 | tf_op jit(solution)/shard_map/ppermute | solution.py:165
  9.2 5.7 %collective-permute-start.6 = (f32[3,32,256]{2,1,0:T(8,128)}, f32[3,32,256]{2,1,0:T(8,128)S(1)}, u32[]{:S(2)}, u32[]{:S(2)}) collective-permute-start(f32[3,32,256]{2,1,0:T(8,128)} %refs_0_.2), channel_id=1, source_target_pairs={{0,24},{4,28},{8,16},{12,20},{16,8},{20,12},{24,0},{28,4},{1,25},{... | collective-permute-start | bytes 294920 | tf_op jit(solution)/shard_map/ppermute | solution.py:165
  10.6 0.7 %copy-start.2 = (f32[64,32]{0,1:T(8,128)S(1)}, f32[64,32]{0,1:T(8,128)}, u32[]{:S(2)}) copy-start(f32[64,32]{0,1:T(8,128)} %param.5) | copy-start | bytes 24580
  11.3 3.6 %copy-start = (f32[3,32,256]{2,1,0:T(8,128)S(1)}, f32[3,32,256]{2,1,0:T(8,128)}, u32[]{:S(2)}) copy-start(f32[3,32,256]{2,1,0:T(8,128)} %refs_0_.2) | copy-start | bytes 294916
  11.3 4.0 %collective-permute-start.7 = (f32[2,32,64]{2,1,0:T(8,128)S(1)}, f32[2,32,64]{2,1,0:T(8,128)S(1)}, u32[]{:S(2)}, u32[]{:S(2)}) collective-permute-start(f32[2,32,64]{2,1,0:T(8,128)S(1)} %get-tuple-element.15.first_ref), channel_id=1, source_target_pairs={{0,16},{4,20},{8,24},{12,28},{16,0},{20,4},{24,8},{28,12},{1,17},{... | collective-permute-start | bytes 49160 | tf_op jit(solution)/shard_map/ppermute | solution.py:165
  12.9 4.6 %collective-permute-start.3 = (f32[3,32,256]{2,1,0:T(8,128)S(1)}, f32[3,32,256]{2,1,0:T(8,128)S(1)}, u32[]{:S(2)}, u32[]{:S(2)}) collective-permute-start(f32[3,32,256]{2,1,0:T(8,128)S(1)} %get-tuple-element.14.refs_4_.refs_1_), channel_id=1, source_target_pairs={{0,1},{1,0},{2,3},{3,2},{4,5},{5,4},{6,7},{7,6},{8,9},{9,8},{10,11... | collective-permute-start | bytes 294920 | tf_op jit(solution)/shard_map/ppermute | solution.py:165
  14.9 2.6 %copy-start.1 = (f32[3,32,256]{2,1,0:T(8,128)S(1)}, f32[3,32,256]{2,1,0:T(8,128)}, u32[]{:S(2)}) copy-start(f32[3,32,256]{2,1,0:T(8,128)} %refs_0_.3) | copy-start | bytes 294916
  14.9 4.0 %collective-permute-start.8 = (f32[4,3,32,256]{3,2,1,0:T(8,128)S(1)}, f32[4,3,32,256]{3,2,1,0:T(8,128)S(1)}, u32[]{:S(2)}, u32[]{:S(2)}) collective-permute-start(f32[4,3,32,256]{3,2,1,0:T(8,128)S(1)} %columns.1.refs_4_), channel_id=1, source_target_pairs={{0,4},{4,0},{8,12},{12,8},{16,20},{20,16},{24,28},{28,24},{1,5},{5... | collective-permute-start | bytes 1179656 | tf_op jit(solution)/shard_map/ppermute | solution.py:165
  15.3 3.6 %collective-permute-start.9 = (f32[4,32,64]{2,1,0:T(8,128)S(1)}, f32[4,32,64]{2,1,0:T(8,128)S(1)}, u32[]{:S(2)}, u32[]{:S(2)}) collective-permute-start(f32[4,32,64]{2,1,0:T(8,128)S(1)} %vectors.3.refs_5_), channel_id=1, source_target_pairs={{0,4},{4,0},{8,12},{12,8},{16,20},{20,16},{24,28},{28,24},{1,5},{5... | collective-permute-start | bytes 98312 | tf_op jit(solution)/shard_map/ppermute | solution.py:165
  20.3 5.7 %collective-permute-start.10 = (f32[32,128]{1,0:T(8,128)S(1)}, f32[32,128]{1,0:T(8,128)S(1)}, u32[]{:S(2)}, u32[]{:S(2)}) collective-permute-start(f32[32,128]{1,0:T(8,128)S(1)} %get-tuple-element.20), channel_id=1, source_target_pairs={{0,3},{1,2},{2,1},{3,0},{4,7},{5,6},{6,5},{7,4},{8,11},{9,10},{10,... | collective-permute-start | bytes 49160 | tf_op jit(solution)/shard_map/ppermute | solution.py:165
  22.9 4.6 %collective-permute-start.11 = (f32[32,128]{1,0:T(8,128)S(1)}, f32[32,128]{1,0:T(8,128)S(1)}, u32[]{:S(2)}, u32[]{:S(2)}) collective-permute-start(f32[32,128]{1,0:T(8,128)S(1)} %get-tuple-element.21), channel_id=1, source_target_pairs={{0,2},{1,3},{2,0},{3,1},{4,6},{5,7},{6,4},{7,5},{8,10},{9,11},{10,... | collective-permute-start | bytes 49160 | tf_op jit(solution)/shard_map/ppermute | solution.py:165
  22.9 4.6 %collective-permute-start.12 = (f32[32,128]{1,0:T(8,128)S(1)}, f32[32,128]{1,0:T(8,128)S(1)}, u32[]{:S(2)}, u32[]{:S(2)}) collective-permute-start(f32[32,128]{1,0:T(8,128)S(1)} %get-tuple-element.22), channel_id=1, source_target_pairs={{0,1},{1,0},{2,3},{3,2},{4,5},{5,4},{6,7},{7,6},{8,9},{9,8},{10,11... | collective-permute-start | bytes 49160 | tf_op jit(solution)/shard_map/ppermute | solution.py:165
where the time goes:
time: 28.5 us; the launch traced here: 28.3 us
  starting transfers between devices  17.4 us (61%)
  waiting for transfers between devices  6.61 us (23%)
  Pallas kernels  3.43 us (12%)
  local copies, waits for them, and re-layouts  0.73 us (3%)
    ppermute x13, starting transfers between devices, exchange(): return lax.ppermute(x, axis, [(at, at ^ mask) for at in range(count)])  17.4 us
    ppermute x13, waiting for transfers between devices, exchange(): return lax.ppermute(x, axis, [(at, at ^ mask) for at in range(count)])  6.61 us
    pallas_call x7, Pallas kernels, call(): pl.pallas_call(kernel, out_shape=out_shape, in_specs=[VM] * len(ins), out...  3.43 us
    unnamed x6, local copies, waits for them, and re-layouts  0.73 us
  transfers between devices with their start and end apart: 13, of which 6 were waited for; matrix products, arithmetic and copies ran while one was open for 0% of the time, Pallas kernels for 5%

commit v1 on v0

--- a/solution.py
+++ b/solution.py
@@ -37,6 +37,10 @@
 def after_far_kernel(far_ref, vec_ref, got_ref, far_out, vec_out):
     far_out[...] = far_ref[...]
     join_kernel(vec_ref, got_ref, vec_out)
+
+
+def pass_kernel(in_ref, *refs):
+    refs[-1][...] = in_ref[...]
 
 
 def columns_kernel(n_blocks, *refs):
@@ -205,6 +209,7 @@
     for mask in col_masks:
         col_order = col_order + [slot ^ mask for slot in col_order]
     cols = [col_frames] + [exchange(col_frames, "row", mask, n_row) for mask in col_order[1:]]
+    (vecs,) = call(pass_kernel, [((2, frames, nv), f32)], [vecs, rows[row_masks[1]]], "vectors")
     for mask in col_masks[1:]:
         got = exchange(vecs, "row", mask, n_row)
         (vecs,) = call(join_kernel, [((2 * vecs.shape[0], frames, nv), f32)], [vecs, got], "vectors")

time: 28.5 us -> 27.1 us (0.951)
  waiting for transfers between devices: 6.61 us -> 5.42 us
    ppermute x13, waiting for transfers between devices: 6.61 us -> 5.42 us  [exchange(): return lax.ppermute(x, axis, [(at, at ^ mask) for at in range(count)])]
    pallas_call x7 -> x8, Pallas kernels: 3.43 us -> 3.44 us  [call(): pl.pallas_call(kernel, out_shape=out_shape, in_specs=[VM] * len(ins), out...]
where the time goes in v1:
time: 27.1 us; the launch traced here: 26.8 us
  starting transfers between devices  17.2 us (63%)
  waiting for transfers between devices  5.42 us (20%)
  Pallas kernels  3.44 us (13%)
  local copies, waits for them, and re-layouts  0.73 us (3%)
    ppermute x13, starting transfers between devices, exchange(): return lax.ppermute(x, axis, [(at, at ^ mask) for at in range(count)])  17.2 us
    ppermute x13, waiting for transfers between devices, exchange(): return lax.ppermute(x, axis, [(at, at ^ mask) for at in range(count)])  5.42 us
    pallas_call x8, Pallas kernels, call(): pl.pallas_call(kernel, out_shape=out_shape, in_specs=[VM] * len(ins), out...  3.44 us
    unnamed x6, local copies, waits for them, and re-layouts  0.73 us
  transfers between devices with their start and end apart: 13, of which 6 were waited for; matrix products, arithmetic and copies ran while one was open for 0% of the time, Pallas kernels for 5%

profile of v1, /device:TPU:0, one launch (start us, length us, event | category | flops | bytes accessed | tf_op | source)
XLA Modules:
  0.0 26.8 jit_solution(5987909624183727909)
XLA Ops:
  0.0 2.9 %collective-permute-start.1 = (f32[1,32,64]{2,1,0:T(8,128)}, f32[1,32,64]{2,1,0:T(8,128)S(1)}, u32[]{:S(2)}, u32[]{:S(2)}) collective-permute-start(f32[1,32,64]{2,1,0:T(8,128)} %bitcast.4), channel_id=1, source_target_pairs={{0,8},{4,12},{8,0},{12,4},{16,24},{20,28},{24,16},{28,20},{1,9},{5... | collective-permute-start | bytes 24584 | tf_op jit(solution)/shard_map/ppermute | solution.py:169
  2.9 2.6 %collective-permute-start = (f32[3,32,256]{2,1,0:T(8,128)}, f32[3,32,256]{2,1,0:T(8,128)S(1)}, u32[]{:S(2)}, u32[]{:S(2)}) collective-permute-start(f32[3,32,256]{2,1,0:T(8,128)} %refs_0_.3), channel_id=1, source_target_pairs={{0,2},{1,3},{2,0},{3,1},{4,6},{5,7},{6,4},{7,5},{8,10},{9,11},{10,... | collective-permute-start | bytes 294920 | tf_op jit(solution)/shard_map/ppermute | solution.py:169
  5.5 1.6 %collective-permute-start.2 = (f32[3,32,256]{2,1,0:T(8,128)}, f32[3,32,256]{2,1,0:T(8,128)S(1)}, u32[]{:S(2)}, u32[]{:S(2)}) collective-permute-start(f32[3,32,256]{2,1,0:T(8,128)} %refs_0_.3), channel_id=1, source_target_pairs={{0,1},{1,0},{2,3},{3,2},{4,5},{5,4},{6,7},{7,6},{8,9},{9,8},{10,11... | collective-permute-start | bytes 294920 | tf_op jit(solution)/shard_map/ppermute | solution.py:169
  7.1 1.5 %collective-permute-start.5 = (f32[3,32,256]{2,1,0:T(8,128)}, f32[3,32,256]{2,1,0:T(8,128)S(1)}, u32[]{:S(2)}, u32[]{:S(2)}) collective-permute-start(f32[3,32,256]{2,1,0:T(8,128)} %refs_0_.2), channel_id=1, source_target_pairs={{0,16},{4,20},{8,24},{12,28},{16,0},{20,4},{24,8},{28,12},{1,17},{... | collective-permute-start | bytes 294920 | tf_op jit(solution)/shard_map/ppermute | solution.py:169
  8.6 0.5 %collective-permute-start.4 = (f32[3,32,256]{2,1,0:T(8,128)}, f32[3,32,256]{2,1,0:T(8,128)S(1)}, u32[]{:S(2)}, u32[]{:S(2)}) collective-permute-start(f32[3,32,256]{2,1,0:T(8,128)} %refs_0_.2), channel_id=1, source_target_pairs={{0,8},{4,12},{8,0},{12,4},{16,24},{20,28},{24,16},{28,20},{1,9},{5... | collective-permute-start | bytes 294920 | tf_op jit(solution)/shard_map/ppermute | solution.py:169
  9.2 0.0 collective-permute-done.1.got_ref
  9.2 1.4 %collective-permute-start.6 = (f32[3,32,256]{2,1,0:T(8,128)}, f32[3,32,256]{2,1,0:T(8,128)S(1)}, u32[]{:S(2)}, u32[]{:S(2)}) collective-permute-start(f32[3,32,256]{2,1,0:T(8,128)} %refs_0_.2), channel_id=1, source_target_pairs={{0,24},{4,28},{8,16},{12,20},{16,8},{20,12},{24,0},{28,4},{1,25},{... | collective-permute-start | bytes 294920 | tf_op jit(solution)/shard_map/ppermute | solution.py:169
  10.6 0.7 %copy-done.2 = f32[64,32]{0,1:T(8,128)S(1)} copy-done((f32[64,32]{0,1:T(8,128)S(1)}, f32[64,32]{0,1:T(8,128)}, u32[]{:S(2)}) %copy-start.2) | copy-done | bytes 8216
  11.3 0.0 collective-permute-done.far_ref
  11.3 0.0 copy-start
  11.3 0.5 %collective-permute-start.3 = (f32[3,32,256]{2,1,0:T(8,128)S(1)}, f32[3,32,256]{2,1,0:T(8,128)S(1)}, u32[]{:S(2)}, u32[]{:S(2)}) collective-permute-start(f32[3,32,256]{2,1,0:T(8,128)S(1)} %get-tuple-element.14.refs_4_.refs_1_), channel_id=1, source_target_pairs={{0,1},{1,0},{2,3},{3,2},{4,5},{5,4},{6,7},{7,6},{8,9},{9,8},{10,11... | collective-permute-start | bytes 294920 | tf_op jit(solution)/shard_map/ppermute | solution.py:169
  11.9 0.0 collective-permute-done.2.refs_5_.refs_0_.refs_2_
  11.9 1.5 %collective-permute-start.7 = (f32[2,32,64]{2,1,0:T(8,128)S(1)}, f32[2,32,64]{2,1,0:T(8,128)S(1)}, u32[]{:S(2)}, u32[]{:S(2)}) collective-permute-start(f32[2,32,64]{2,1,0:T(8,128)S(1)} %vectors.4.first_ref), channel_id=1, source_target_pairs={{0,16},{4,20},{8,24},{12,28},{16,0},{20,4},{24,8},{28,12},{1,17},{... | collective-permute-start | bytes 49160 | tf_op jit(solution)/shard_map/ppermute | solution.py:169
  13.4 0.0 collective-permute-done.5.refs_2_
  13.4 0.1 collective-permute-done.4.refs_1_
  13.5 1.4 %collective-permute-done.6.refs_3_ = f32[3,32,256]{2,1,0:T(8,128)S(1)} collective-permute-done((f32[3,32,256]{2,1,0:T(8,128)}, f32[3,32,256]{2,1,0:T(8,128)S(1)}, u32[]{:S(2)}, u32[]{:S(2)}) %collective-permute-start.6) | collective-permute-done | bytes 98336 | tf_op jit(solution)/shard_map/ppermute | solution.py:169
  14.9 0.0 copy-start.1
  14.9 0.1 collective-permute-start.8
  15.0 0.8 %collective-permute-done.7.second_ref = f32[2,32,64]{2,1,0:T(8,128)S(1)} collective-permute-done((f32[2,32,64]{2,1,0:T(8,128)S(1)}, f32[2,32,64]{2,1,0:T(8,128)S(1)}, u32[]{:S(2)}, u32[]{:S(2)}) %collective-permute-start.7) | collective-permute-done | bytes 16416 | tf_op jit(solution)/shard_map/ppermute | solution.py:169
  15.8 0.0 collective-permute-start.9
  15.8 0.2 collective-permute-done.3.refs_3_
  16.0 1.4 %first_tile.1 = (f32[1,128,128]{2,1,0:T(8,128)S(1)}, bf16[1,384,768]{2,1,0:T(8,128)(2,1)S(1)}, f32[1,128,128]{2,1,0:T(8,128)S(1)}) custom-call(f32[3,32,256]{2,1,0:T(8,128)S(1)} %copy-done.1, f32[3,32,256]{2,1,0:T(8,128)S(1)} %get-tuple-element.14.refs_4_.refs_1_, f32[3,32,256]{2,1,0:T(8,128)S(1)} %collective-permute-done.2.refs_5_.refs_0_.refs_2_, ...), custom_call_target="tpu_custom_call" | custom-call | flops 57982058496 | bytes 819200 | tf_op jit(solution)/shard_map/first_tile/pallas_call | solution.py:175
  17.4 0.0 collective-permute-done.9.vecs_ref
  17.4 0.0 collective-permute-done.8.blocks_ref
  17.4 1.3 %second_tile.1 = (f32[32,128]{1,0:T(8,128)S(1)}, f32[32,128]{1,0:T(8,128)S(1)}, f32[32,128]{1,0:T(8,128)S(1)}, f32[32,128]{1,0:T(8,128)S(1)}) custom-call(f32[1,128,128]{2,1,0:T(8,128)S(1)} %get-tuple-element.16.sum_ref, bf16[1,384,768]{2,1,0:T(8,128)(2,1)S(1)} %get-tuple-element.17.side_ref, f32[1,128,128]{2,1,0:T(8,128)S(1)} %get-tuple-element.18.norm_ref, ...), custom_call_target="tpu_custom_call" | custom-call | flops 226492416 | bytes 1736704 | tf_op jit(solution)/shard_map/second_tile/pallas_call | solution.py:175
  18.8 2.6 %collective-permute-start.10 = (f32[32,128]{1,0:T(8,128)S(1)}, f32[32,128]{1,0:T(8,128)S(1)}, u32[]{:S(2)}, u32[]{:S(2)}) collective-permute-start(f32[32,128]{1,0:T(8,128)S(1)} %get-tuple-element.20), channel_id=1, source_target_pairs={{0,3},{1,2},{2,1},{3,0},{4,7},{5,6},{6,5},{7,4},{8,11},{9,10},{10,... | collective-permute-start | bytes 49160 | tf_op jit(solution)/shard_map/ppermute | solution.py:169
  21.4 0.3 collective-permute-start.11
  21.7 1.6 %collective-permute-start.12 = (f32[32,128]{1,0:T(8,128)S(1)}, f32[32,128]{1,0:T(8,128)S(1)}, u32[]{:S(2)}, u32[]{:S(2)}) collective-permute-start(f32[32,128]{1,0:T(8,128)S(1)} %get-tuple-element.22), channel_id=1, source_target_pairs={{0,1},{1,0},{2,3},{3,2},{4,5},{5,4},{6,7},{7,6},{8,9},{9,8},{10,11... | collective-permute-start | bytes 49160 | tf_op jit(solution)/shard_map/ppermute | solution.py:169
  23.2 1.3 %collective-permute-done.10.refs_1_ = f32[32,128]{1,0:T(8,128)S(1)} collective-permute-done((f32[32,128]{1,0:T(8,128)S(1)}, f32[32,128]{1,0:T(8,128)S(1)}, u32[]{:S(2)}, u32[]{:S(2)}) %collective-permute-start.10) | collective-permute-done | bytes 16416 | tf_op jit(solution)/shard_map/ppermute | solution.py:169
  24.5 1.7 %collective-permute-done.11.refs_2_ = f32[32,128]{1,0:T(8,128)S(1)} collective-permute-done((f32[32,128]{1,0:T(8,128)S(1)}, f32[32,128]{1,0:T(8,128)S(1)}, u32[]{:S(2)}, u32[]{:S(2)}) %collective-permute-start.11) | collective-permute-done | bytes 16416 | tf_op jit(solution)/shard_map/ppermute | solution.py:169
  26.1 0.0 collective-permute-done.12.refs_3_
  26.1 0.7 %sum_divide.1 = f32[32,64]{1,0:T(8,128)} custom-call(f32[32,128]{1,0:T(8,128)S(1)} %get-tuple-element.19.refs_0_, f32[32,128]{1,0:T(8,128)S(1)} %collective-permute-done.10.refs_1_, f32[32,128]{1,0:T(8,128)S(1)} %collective-permute-done.11.refs_2_, f32[32,128]{1,0:T(8,128)S(1)} %collective-permute-done.12.refs_3_), custom_call_target="tpu_custom_call" | custom-call | bytes 65536 | tf_op jit(solution)/shard_map/sum_divide/pallas_call | solution.py:175
  (8 shorter events, 0.1 us)
Async XLA Ops:
  0.0 9.2 %collective-permute-start.1 = (f32[1,32,64]{2,1,0:T(8,128)}, f32[1,32,64]{2,1,0:T(8,128)S(1)}, u32[]{:S(2)}, u32[]{:S(2)}) collective-permute-start(f32[1,32,64]{2,1,0:T(8,128)} %bitcast.4), channel_id=1, source_target_pairs={{0,8},{4,12},{8,0},{12,4},{16,24},{20,28},{24,16},{28,20},{1,9},{5... | collective-permute-start | bytes 24584 | tf_op jit(solution)/shard_map/ppermute | solution.py:169
  2.9 8.4 %collective-permute-start = (f32[3,32,256]{2,1,0:T(8,128)}, f32[3,32,256]{2,1,0:T(8,128)S(1)}, u32[]{:S(2)}, u32[]{:S(2)}) collective-permute-start(f32[3,32,256]{2,1,0:T(8,128)} %refs_0_.3), channel_id=1, source_target_pairs={{0,2},{1,3},{2,0},{3,1},{4,6},{5,7},{6,4},{7,5},{8,10},{9,11},{10,... | collective-permute-start | bytes 294920 | tf_op jit(solution)/shard_map/ppermute | solution.py:169
  5.5 6.3 %collective-permute-start.2 = (f32[3,32,256]{2,1,0:T(8,128)}, f32[3,32,256]{2,1,0:T(8,128)S(1)}, u32[]{:S(2)}, u32[]{:S(2)}) collective-permute-start(f32[3,32,256]{2,1,0:T(8,128)} %refs_0_.3), channel_id=1, source_target_pairs={{0,1},{1,0},{2,3},{3,2},{4,5},{5,4},{6,7},{7,6},{8,9},{9,8},{10,11... | collective-permute-start | bytes 294920 | tf_op jit(solution)/shard_map/ppermute | solution.py:169
  7.1 6.3 %collective-permute-start.5 = (f32[3,32,256]{2,1,0:T(8,128)}, f32[3,32,256]{2,1,0:T(8,128)S(1)}, u32[]{:S(2)}, u32[]{:S(2)}) collective-permute-start(f32[3,32,256]{2,1,0:T(8,128)} %refs_0_.2), channel_id=1, source_target_pairs={{0,16},{4,20},{8,24},{12,28},{16,0},{20,4},{24,8},{28,12},{1,17},{... | collective-permute-start | bytes 294920 | tf_op jit(solution)/shard_map/ppermute | solution.py:169
  8.6 4.8 %collective-permute-start.4 = (f32[3,32,256]{2,1,0:T(8,128)}, f32[3,32,256]{2,1,0:T(8,128)S(1)}, u32[]{:S(2)}, u32[]{:S(2)}) collective-permute-start(f32[3,32,256]{2,1,0:T(8,128)} %refs_0_.2), channel_id=1, source_target_pairs={{0,8},{4,12},{8,0},{12,4},{16,24},{20,28},{24,16},{28,20},{1,9},{5... | collective-permute-start | bytes 294920 | tf_op jit(solution)/shard_map/ppermute | solution.py:169
  9.2 5.7 %collective-permute-start.6 = (f32[3,32,256]{2,1,0:T(8,128)}, f32[3,32,256]{2,1,0:T(8,128)S(1)}, u32[]{:S(2)}, u32[]{:S(2)}) collective-permute-start(f32[3,32,256]{2,1,0:T(8,128)} %refs_0_.2), channel_id=1, source_target_pairs={{0,24},{4,28},{8,16},{12,20},{16,8},{20,12},{24,0},{28,4},{1,25},{... | collective-permute-start | bytes 294920 | tf_op jit(solution)/shard_map/ppermute | solution.py:169
  10.6 0.7 %copy-start.2 = (f32[64,32]{0,1:T(8,128)S(1)}, f32[64,32]{0,1:T(8,128)}, u32[]{:S(2)}) copy-start(f32[64,32]{0,1:T(8,128)} %param.5) | copy-start | bytes 24580
  11.3 3.6 %copy-start = (f32[3,32,256]{2,1,0:T(8,128)S(1)}, f32[3,32,256]{2,1,0:T(8,128)}, u32[]{:S(2)}) copy-start(f32[3,32,256]{2,1,0:T(8,128)} %refs_0_.2) | copy-start | bytes 294916
  11.3 4.7 %collective-permute-start.3 = (f32[3,32,256]{2,1,0:T(8,128)S(1)}, f32[3,32,256]{2,1,0:T(8,128)S(1)}, u32[]{:S(2)}, u32[]{:S(2)}) collective-permute-start(f32[3,32,256]{2,1,0:T(8,128)S(1)} %get-tuple-element.14.refs_4_.refs_1_), channel_id=1, source_target_pairs={{0,1},{1,0},{2,3},{3,2},{4,5},{5,4},{6,7},{7,6},{8,9},{9,8},{10,11... | collective-permute-start | bytes 294920 | tf_op jit(solution)/shard_map/ppermute | solution.py:169
  11.9 3.9 %collective-permute-start.7 = (f32[2,32,64]{2,1,0:T(8,128)S(1)}, f32[2,32,64]{2,1,0:T(8,128)S(1)}, u32[]{:S(2)}, u32[]{:S(2)}) collective-permute-start(f32[2,32,64]{2,1,0:T(8,128)S(1)} %vectors.4.first_ref), channel_id=1, source_target_pairs={{0,16},{4,20},{8,24},{12,28},{16,0},{20,4},{24,8},{28,12},{1,17},{... | collective-permute-start | bytes 49160 | tf_op jit(solution)/shard_map/ppermute | solution.py:169
  14.9 1.1 %copy-start.1 = (f32[3,32,256]{2,1,0:T(8,128)S(1)}, f32[3,32,256]{2,1,0:T(8,128)}, u32[]{:S(2)}) copy-start(f32[3,32,256]{2,1,0:T(8,128)} %refs_0_.3) | copy-start | bytes 294916
  14.9 2.5 %collective-permute-start.8 = (f32[4,3,32,256]{3,2,1,0:T(8,128)S(1)}, f32[4,3,32,256]{3,2,1,0:T(8,128)S(1)}, u32[]{:S(2)}, u32[]{:S(2)}) collective-permute-start(f32[4,3,32,256]{3,2,1,0:T(8,128)S(1)} %columns.1.refs_4_), channel_id=1, source_target_pairs={{0,4},{4,0},{8,12},{12,8},{16,20},{20,16},{24,28},{28,24},{1,5},{5... | collective-permute-start | bytes 1179656 | tf_op jit(solution)/shard_map/ppermute | solution.py:169
  15.8 1.6 %collective-permute-start.9 = (f32[4,32,64]{2,1,0:T(8,128)S(1)}, f32[4,32,64]{2,1,0:T(8,128)S(1)}, u32[]{:S(2)}, u32[]{:S(2)}) collective-permute-start(f32[4,32,64]{2,1,0:T(8,128)S(1)} %vectors.5.refs_5_), channel_id=1, source_target_pairs={{0,4},{4,0},{8,12},{12,8},{16,20},{20,16},{24,28},{28,24},{1,5},{5... | collective-permute-start | bytes 98312 | tf_op jit(solution)/shard_map/ppermute | solution.py:169
  18.8 5.7 %collective-permute-start.10 = (f32[32,128]{1,0:T(8,128)S(1)}, f32[32,128]{1,0:T(8,128)S(1)}, u32[]{:S(2)}, u32[]{:S(2)}) collective-permute-start(f32[32,128]{1,0:T(8,128)S(1)} %get-tuple-element.20), channel_id=1, source_target_pairs={{0,3},{1,2},{2,1},{3,0},{4,7},{5,6},{6,5},{7,4},{8,11},{9,10},{10,... | collective-permute-start | bytes 49160 | tf_op jit(solution)/shard_map/ppermute | solution.py:169
  21.4 4.7 %collective-permute-start.11 = (f32[32,128]{1,0:T(8,128)S(1)}, f32[32,128]{1,0:T(8,128)S(1)}, u32[]{:S(2)}, u32[]{:S(2)}) collective-permute-start(f32[32,128]{1,0:T(8,128)S(1)} %get-tuple-element.21), channel_id=1, source_target_pairs={{0,2},{1,3},{2,0},{3,1},{4,6},{5,7},{6,4},{7,5},{8,10},{9,11},{10,... | collective-permute-start | bytes 49160 | tf_op jit(solution)/shard_map/ppermute | solution.py:169
  21.7 4.5 %collective-permute-start.12 = (f32[32,128]{1,0:T(8,128)S(1)}, f32[32,128]{1,0:T(8,128)S(1)}, u32[]{:S(2)}, u32[]{:S(2)}) collective-permute-start(f32[32,128]{1,0:T(8,128)S(1)} %get-tuple-element.22), channel_id=1, source_target_pairs={{0,1},{1,0},{2,3},{3,2},{4,5},{5,4},{6,7},{7,6},{8,9},{9,8},{10,11... | collective-permute-start | bytes 49160 | tf_op jit(solution)/shard_map/ppermute | solution.py:169

commit v2 on v1

--- a/solution.py
+++ b/solution.py
@@ -95,9 +95,8 @@
     return jnp.exp(-squared / BAND)
 
 
-def column_side(blocks_ref, vecs_ref):
-    count, _, frames, atoms = blocks_ref.shape
-    nv = vecs_ref.shape[2]
+def column_side(blocks_ref):
+    count, _, _, atoms = blocks_ref.shape
     cols = [
         centre(jnp.concatenate([blocks_ref[at, comp] for at in range(count)], axis=0)) for comp in range(3)
     ]
@@ -105,57 +104,84 @@
     norm = lax.dot_general(
         jnp.ones((8, atoms), jnp.float32), col_square, NT,
         precision=lax.Precision.HIGHEST, preferred_element_type=jnp.float32,
-    )[0:1, :]
+    )
     high, low = split(jnp.concatenate(cols, axis=0))
-    side = jnp.concatenate([high, high, low], axis=1)
+    return jnp.concatenate([high, high, low], axis=1), norm
+
+
+def vector_side(vecs_ref):
+    count, frames, nv = vecs_ref.shape
     ones = jnp.where(lax.broadcasted_iota(jnp.int32, (count * frames, LANES - nv), 1) == 0, 1.0, 0.0)
     vecs = jnp.concatenate([vecs_ref[at] for at in range(count)], axis=0)
     high, low = split(jnp.concatenate([vecs, ones], axis=1))
-    return side, norm, jnp.concatenate([high, high, low], axis=0)
-
-
-def multiply(row_side, row_norm, side, norm, vec, atoms, moment, tile):
+    return [high, high, low]
+
+
+def row_side(slots):
+    rows = [centre(jnp.concatenate([ref[comp] for ref in slots], axis=0)) for comp in range(3)]
+    square = jnp.sum(rows[0] * rows[0] + rows[1] * rows[1] + rows[2] * rows[2], axis=1, keepdims=True)
+    high, low = split(jnp.concatenate(rows, axis=0))
+    return jnp.concatenate([high, low, high], axis=1), jnp.broadcast_to(square, (square.shape[0], LANES))
+
+
+def kernel_tile(rows, row_norm, side, norm, moment, tile):
     count = row_norm.shape[0]
     count_cols = norm.shape[1]
-    moment[...] = lax.dot_general(row_side, side, NT, preferred_element_type=jnp.float32)
+    atoms = side.shape[1] // 3
+    moment[0:3 * count, :] = lax.dot_general(rows, side, NT, preferred_element_type=jnp.float32)
     for at in range(0, count, 8):
         m = [
             moment[a * count + at:a * count + at + 8, b * count_cols:(b + 1) * count_cols]
             for a in range(3) for b in range(3)
         ]
-        half_norm = 0.5 * (row_norm[at:at + 8, 0:1] + norm)
+        half_norm = 0.5 * (row_norm[at:at + 8, 0:1] + norm[0:1, :])
         tile[at:at + 8, :] = eigen_tile(m, half_norm, atoms)
-    high, low = split(tile[...])
-    return jnp.dot(jnp.concatenate([high, low, high], axis=1), vec, preferred_element_type=jnp.float32)
-
-
-def first_kernel(n_mine, *refs):
-    slots, blocks_ref, vecs_ref = refs[:n_mine], refs[n_mine], refs[n_mine + 1]
-    sum_ref, side_ref, norm_ref, moment, tile = refs[n_mine + 2:]
-    _, frames, atoms = slots[0].shape
-    groups, count, _ = sum_ref.shape
-    side, norm, vec = column_side(blocks_ref, vecs_ref)
+
+
+def early_kernel(n_early, *refs):
+    slots, blocks_ref = refs[:n_early], refs[n_early]
+    rows_ref, row_norm_ref, tile_ref, side_ref, norm_ref, moment = refs[n_early + 1:]
+    frames = slots[0].shape[1]
+    groups, count, _ = tile_ref.shape
+    side, norm = column_side(blocks_ref)
+    side_ref[...] = side
+    norm_ref[...] = norm
     for group in range(groups):
         own = slots[group * count // frames:(group + 1) * count // frames]
-        rows = [centre(jnp.concatenate([ref[comp] for ref in own], axis=0)) for comp in range(3)]
-        square = jnp.sum(rows[0] * rows[0] + rows[1] * rows[1] + rows[2] * rows[2], axis=1, keepdims=True)
-        row_norm = jnp.broadcast_to(square, (count, LANES))
-        high, low = split(jnp.concatenate(rows, axis=0))
-        row_side = jnp.concatenate([high, low, high], axis=1)
-        side_ref[group] = row_side
-        norm_ref[group] = row_norm
-        sum_ref[group] = multiply(row_side, row_norm, side, norm, vec, atoms, moment, tile)
-
-
-def second_kernel(frames, sum_ref, side_ref, norm_ref, blocks_ref, vecs_ref, *refs):
-    moment, tile = refs[-2:]
-    atoms = blocks_ref.shape[-1]
-    groups, count, _ = sum_ref.shape
-    side, norm, vec = column_side(blocks_ref, vecs_ref)
+        used = len(own) * frames
+        rows, row_norm = row_side(own)
+        for comp in range(3):
+            rows_ref[group, comp * count:comp * count + used, :] = rows[comp * used:(comp + 1) * used]
+        row_norm_ref[group, 0:used, :] = row_norm
+        kernel_tile(rows, row_norm, side, norm, moment, tile_ref.at[group, 0:used])
+
+
+def last_kernel(row_ref, side_ref, norm_ref, *refs):
+    rows_ref, row_norm_ref, tile_ref, moment = refs[3:]
+    frames = row_ref.shape[1]
+    groups, count, _ = tile_ref.shape
+    rows, row_norm = row_side([row_ref])
+    for comp in range(3):
+        rows_ref[groups - 1, (comp + 1) * count - frames:(comp + 1) * count, :] = rows[comp * frames:(comp + 1) * frames]
+    row_norm_ref[groups - 1, count - frames:, :] = row_norm
+    kernel_tile(rows, row_norm, side_ref[...], norm_ref[...], moment, tile_ref.at[groups - 1, count - frames:count])
+
+
+def second_kernel(frames, rows_ref, row_norm_ref, tile_ref, vecs_ref, blocks_ref, other_vecs_ref, *refs):
+    out_refs, moment, other_tile = refs[:-2], refs[-2], refs[-1]
+    groups, count, _ = tile_ref.shape
+    side, norm = column_side(blocks_ref)
+    vecs = jnp.concatenate(vector_side(vecs_ref) + vector_side(other_vecs_ref), axis=0)
     for group in range(groups):
-        total = sum_ref[group] + multiply(side_ref[group], norm_ref[group], side, norm, vec, atoms, moment, tile)
+        kernel_tile(rows_ref[group], row_norm_ref[group], side, norm, moment, other_tile)
+        high, low = split(tile_ref[group])
+        other_high, other_low = split(other_tile[...])
+        total = jnp.dot(
+            jnp.concatenate([high, low, high, other_high, other_low, other_high], axis=1), vecs,
+            preferred_element_type=jnp.float32,
+        )
         for at in range(count // frames):
-            refs[group * count // frames + at][...] = total[at * frames:(at + 1) * frames, :]
+            out_refs[group * count // frames + at][...] = total[at * frames:(at + 1) * frames, :]
 
 
 def finish_kernel(nv, *refs):
@@ -169,7 +195,7 @@
     return lax.ppermute(x, axis, [(at, at ^ mask) for at in range(count)])
 
 
-def call(kernel, outs, ins, name, scratch=(), megabytes=8, flops=0):
+def call(kernel, outs, ins, name, scratch=(), megabytes=8, flops=0, aliases=None):
     out_shape = [jax.ShapeDtypeStruct(*out) for out in outs]
     moved = sum(x.size * 4 for x in ins)
     return pl.pallas_call(
@@ -178,6 +204,7 @@
         in_specs=[VM] * len(ins),
         out_specs=[VM] * len(outs),
         scratch_shapes=list(scratch),
+        input_output_aliases=aliases or {},
         compiler_params=pltpu.CompilerParams(vmem_limit_bytes=megabytes * 1024 * 1024),
         cost_estimate=pl.CostEstimate(flops=flops, bytes_accessed=moved, transcendentals=0),
         name=name,
@@ -223,16 +250,24 @@
     half_cols = n_row // 2 * frames
     count = min(n_col, max(1, LANES // frames)) * frames
     groups = n_col * frames // count
-    scratch = [pltpu.VMEM((3 * count, 3 * half_cols), f32), pltpu.VMEM((count, half_cols), f32)]
+    moment = pltpu.VMEM((3 * count, 3 * half_cols), f32)
+    tile = pltpu.VMEM((count, half_cols), f32)
     work = 2 * 3 * n_col * frames * 3 * half_cols * 3 * atoms
-    sums, side, norm = call(
-        functools.partial(first_kernel, n_col),
-        [((groups, count, LANES), f32), ((groups, 3 * count, 3 * atoms), bf16), ((groups, count, LANES), f32)],
-        [*[rows[slot] for slot in order], blocks, vecs], "first_tile", scratch, 32, work << 8,
+    outs = [
+        ((groups, 3 * count, 3 * atoms), bf16), ((groups, count, LANES), f32), ((groups, count, half_cols), f32),
+    ]
+    *kept, side, norm = call(
+        functools.partial(early_kernel, n_col - 1),
+        outs + [((3 * half_cols, 3 * atoms), bf16), ((8, half_cols), f32)],
+        [*[rows[slot] for slot in order[:-1]], blocks], "early_tile", [moment], 32, work,
+    )
+    kept = call(
+        last_kernel, outs, [rows[order[-1]], side, norm, *kept], "last_tile",
+        [pltpu.VMEM((3 * frames, 3 * half_cols), f32)], 32, work << 8, {3: 0, 4: 1, 5: 2},
     )
     parts = call(
         functools.partial(second_kernel, frames), [((frames, LANES), f32)] * n_col,
-        [sums, side, norm, other, other_vecs], "second_tile", scratch, 32, work,
+        [*kept, vecs, other, other_vecs], "second_tile", [moment, tile], 32, work,
     )
     shares = [parts[0]] + [
         exchange(parts[order.index(mask)], "col", mask, n_col) for mask in range(n_col - 1, 0, -1)

time: 27.1 us -> 26.5 us (0.978)
  waiting for transfers between devices: 5.42 us -> 3.94 us
  starting transfers between devices: 17.2 us -> 17.8 us
    ppermute x13, waiting for transfers between devices: 5.42 us -> 3.94 us  [exchange(): return lax.ppermute(x, axis, [(at, at ^ mask) for at in range(count)])]
    ppermute x13, starting transfers between devices: 17.2 us -> 17.8 us  [exchange(): return lax.ppermute(x, axis, [(at, at ^ mask) for at in range(count)])]
    pallas_call x8 -> x9, Pallas kernels: 3.44 us -> 3.7 us  [call(): pl.pallas_call(kernel, out_shape=out_shape, in_specs=[VM] * len(ins), out...]
  transfers between devices with their start and end apart: 13 -> 13, of which waited for: 6 -> 4; matrix products, arithmetic and copies ran while one was open for 0% -> 0% of each run, Pallas kernels for 5% -> 6%
where the time goes in v2:
time: 26.5 us; the launch traced here: 26.2 us
  starting transfers between devices  17.8 us (67%)
  waiting for transfers between devices  3.94 us (15%)
  Pallas kernels  3.7 us (14%)
  local copies, waits for them, and re-layouts  0.73 us (3%)
    ppermute x13, starting transfers between devices, exchange(): return lax.ppermute(x, axis, [(at, at ^ mask) for at in range(count)])  17.8 us
    ppermute x13, waiting for transfers between devices, exchange(): return lax.ppermute(x, axis, [(at, at ^ mask) for at in range(count)])  3.94 us
    pallas_call x9, Pallas kernels, call(): pl.pallas_call(kernel, out_shape=out_shape, in_specs=[VM] * len(ins), out...  3.7 us
    unnamed x6, local copies, waits for them, and re-layouts  0.73 us
  transfers between devices with their start and end apart: 13, of which 4 were waited for; matrix products, arithmetic and copies ran while one was open for 0% of the time, Pallas kernels for 6%

profile of v2, /device:TPU:0, one launch (start us, length us, event | category | flops | bytes accessed | tf_op | source)
XLA Modules:
  0.0 26.2 jit_solution(12840528909161564228)
XLA Ops:
  0.0 2.9 %collective-permute-start.1 = (f32[1,32,64]{2,1,0:T(8,128)}, f32[1,32,64]{2,1,0:T(8,128)S(1)}, u32[]{:S(2)}, u32[]{:S(2)}) collective-permute-start(f32[1,32,64]{2,1,0:T(8,128)} %bitcast.4), channel_id=1, source_target_pairs={{0,8},{4,12},{8,0},{12,4},{16,24},{20,28},{24,16},{28,20},{1,9},{5... | collective-permute-start | bytes 24584 | tf_op jit(solution)/shard_map/ppermute | solution.py:195
  2.9 2.6 %collective-permute-start = (f32[3,32,256]{2,1,0:T(8,128)}, f32[3,32,256]{2,1,0:T(8,128)S(1)}, u32[]{:S(2)}, u32[]{:S(2)}) collective-permute-start(f32[3,32,256]{2,1,0:T(8,128)} %refs_0_.3), channel_id=1, source_target_pairs={{0,2},{1,3},{2,0},{3,1},{4,6},{5,7},{6,4},{7,5},{8,10},{9,11},{10,... | collective-permute-start | bytes 294920 | tf_op jit(solution)/shard_map/ppermute | solution.py:195
  5.5 1.6 %collective-permute-start.3 = (f32[3,32,256]{2,1,0:T(8,128)}, f32[3,32,256]{2,1,0:T(8,128)S(1)}, u32[]{:S(2)}, u32[]{:S(2)}) collective-permute-start(f32[3,32,256]{2,1,0:T(8,128)} %refs_0_.3), channel_id=1, source_target_pairs={{0,1},{1,0},{2,3},{3,2},{4,5},{5,4},{6,7},{7,6},{8,9},{9,8},{10,11... | collective-permute-start | bytes 294920 | tf_op jit(solution)/shard_map/ppermute | solution.py:195
  7.1 1.5 %collective-permute-start.5 = (f32[3,32,256]{2,1,0:T(8,128)}, f32[3,32,256]{2,1,0:T(8,128)S(1)}, u32[]{:S(2)}, u32[]{:S(2)}) collective-permute-start(f32[3,32,256]{2,1,0:T(8,128)} %refs_0_.2), channel_id=1, source_target_pairs={{0,16},{4,20},{8,24},{12,28},{16,0},{20,4},{24,8},{28,12},{1,17},{... | collective-permute-start | bytes 294920 | tf_op jit(solution)/shard_map/ppermute | solution.py:195
  8.6 0.5 %collective-permute-start.4 = (f32[3,32,256]{2,1,0:T(8,128)}, f32[3,32,256]{2,1,0:T(8,128)S(1)}, u32[]{:S(2)}, u32[]{:S(2)}) collective-permute-start(f32[3,32,256]{2,1,0:T(8,128)} %refs_0_.2), channel_id=1, source_target_pairs={{0,8},{4,12},{8,0},{12,4},{16,24},{20,28},{24,16},{28,20},{1,9},{5... | collective-permute-start | bytes 294920 | tf_op jit(solution)/shard_map/ppermute | solution.py:195
  9.2 0.0 collective-permute-done.1.got_ref
  9.2 1.4 %collective-permute-start.6 = (f32[3,32,256]{2,1,0:T(8,128)}, f32[3,32,256]{2,1,0:T(8,128)S(1)}, u32[]{:S(2)}, u32[]{:S(2)}) collective-permute-start(f32[3,32,256]{2,1,0:T(8,128)} %refs_0_.2), channel_id=1, source_target_pairs={{0,24},{4,28},{8,16},{12,20},{16,8},{20,12},{24,0},{28,4},{1,25},{... | collective-permute-start | bytes 294920 | tf_op jit(solution)/shard_map/ppermute | solution.py:195
  10.6 0.7 %copy-done.2 = f32[64,32]{0,1:T(8,128)S(1)} copy-done((f32[64,32]{0,1:T(8,128)S(1)}, f32[64,32]{0,1:T(8,128)}, u32[]{:S(2)}) %copy-start.2) | copy-done | bytes 8216
  11.3 0.0 collective-permute-done.far_ref
  11.3 0.0 copy-start
  11.3 0.5 %collective-permute-start.2 = (f32[3,32,256]{2,1,0:T(8,128)S(1)}, f32[3,32,256]{2,1,0:T(8,128)S(1)}, u32[]{:S(2)}, u32[]{:S(2)}) collective-permute-start(f32[3,32,256]{2,1,0:T(8,128)S(1)} %get-tuple-element.19.refs_4_.refs_1_), channel_id=1, source_target_pairs={{0,1},{1,0},{2,3},{3,2},{4,5},{5,4},{6,7},{7,6},{8,9},{9,8},{10,11... | collective-permute-start | bytes 294920 | tf_op jit(solution)/shard_map/ppermute | solution.py:195
  11.9 0.0 collective-permute-done.3.refs_5_.refs_2_.refs_0_
  11.9 1.6 %collective-permute-start.7 = (f32[2,32,64]{2,1,0:T(8,128)S(1)}, f32[2,32,64]{2,1,0:T(8,128)S(1)}, u32[]{:S(2)}, u32[]{:S(2)}) collective-permute-start(f32[2,32,64]{2,1,0:T(8,128)S(1)} %vectors.4.first_ref), channel_id=1, source_target_pairs={{0,16},{4,20},{8,24},{12,28},{16,0},{20,4},{24,8},{28,12},{1,17},{... | collective-permute-start | bytes 49160 | tf_op jit(solution)/shard_map/ppermute | solution.py:195
  13.5 0.0 collective-permute-done.5.refs_2_
  13.5 0.0 collective-permute-done.4.refs_1_
  13.5 1.4 %collective-permute-done.6.refs_3_ = f32[3,32,256]{2,1,0:T(8,128)S(1)} collective-permute-done((f32[3,32,256]{2,1,0:T(8,128)}, f32[3,32,256]{2,1,0:T(8,128)S(1)}, u32[]{:S(2)}, u32[]{:S(2)}) %collective-permute-start.6) | collective-permute-done | bytes 98336 | tf_op jit(solution)/shard_map/ppermute | solution.py:195
  14.9 0.1 collective-permute-start.8
  15.0 1.1 %early_tile.1 = (bf16[1,384,768]{2,1,0:T(8,128)(2,1)S(1)}, f32[1,128,128]{2,1,0:T(8,128)S(1)}, f32[1,128,128]{2,1,0:T(8,128)S(1)}, bf16[384,768]{1,0:T(8,128)(2,1)S(1)}, f32[8,128]{1,0:T(8,128)S(1)}) custom-call(f32[3,32,256]{2,1,0:T(8,128)S(1)} %copy-done.1, f32[3,32,256]{2,1,0:T(8,128)S(1)} %get-tuple-element.19.refs_4_.refs_1_, ...), custom_call_target="tpu_custom_call" | custom-call | flops 226492416 | bytes 688128 | tf_op jit(solution)/shard_map/early_tile/pallas_call | solution.py:201
  16.1 0.0 collective-permute-done.7.second_ref
  16.1 0.6 %collective-permute-start.9 = (f32[4,32,64]{2,1,0:T(8,128)S(1)}, f32[4,32,64]{2,1,0:T(8,128)S(1)}, u32[]{:S(2)}, u32[]{:S(2)}) collective-permute-start(f32[4,32,64]{2,1,0:T(8,128)S(1)} %vectors.5.vecs_ref), channel_id=1, source_target_pairs={{0,4},{4,0},{8,12},{12,8},{16,20},{20,16},{24,28},{28,24},{1,5},{5... | collective-permute-start | bytes 98312 | tf_op jit(solution)/shard_map/ppermute | solution.py:195
  16.7 0.0 collective-permute-done.2.row_ref
  16.7 0.5 %last_tile.1 = (bf16[1,384,768]{2,1,0:T(8,128)(2,1)S(1)}, f32[1,128,128]{2,1,0:T(8,128)S(1)}, f32[1,128,128]{2,1,0:T(8,128)S(1)}) custom-call(f32[3,32,256]{2,1,0:T(8,128)S(1)} %collective-permute-done.2.row_ref, bf16[384,768]{1,0:T(8,128)(2,1)S(1)} %get-tuple-element.20.side_ref, ...), custom_call_target="tpu_custom_call", output_to_operand_aliasing={{0}: (3, {}), {1}: (4, {}), {2}: (5, {})} | custom-call | flops 57982058496 | bytes 2592768 | tf_op jit(solution)/shard_map/last_tile/pallas_call | solution.py:201
  17.2 0.4 %collective-permute-done.9.other_vecs_ref = f32[4,32,64]{2,1,0:T(8,128)S(1)} collective-permute-done((f32[4,32,64]{2,1,0:T(8,128)S(1)}, f32[4,32,64]{2,1,0:T(8,128)S(1)}, u32[]{:S(2)}, u32[]{:S(2)}) %collective-permute-start.9) | collective-permute-done | bytes 32800 | tf_op jit(solution)/shard_map/ppermute | solution.py:195
  17.6 0.0 collective-permute-done.8.blocks_ref
  17.6 1.4 %second_tile.1 = (f32[32,128]{1,0:T(8,128)S(1)}, f32[32,128]{1,0:T(8,128)S(1)}, f32[32,128]{1,0:T(8,128)S(1)}, f32[32,128]{1,0:T(8,128)S(1)}) custom-call(bf16[1,384,768]{2,1,0:T(8,128)(2,1)S(1)} %get-tuple-element.25.rows_ref, f32[1,128,128]{2,1,0:T(8,128)S(1)} %get-tuple-element.26.row_norm_ref, f32[1,128,128]{2,1,0:T(8,128)S(1)} %get-tuple-element.27.tile_ref, ...), custom_call_target="tpu_custom_call" | custom-call | flops 226492416 | bytes 1769472 | tf_op jit(solution)/shard_map/second_tile/pallas_call | solution.py:201
  19.0 1.8 %collective-permute-start.10 = (f32[32,128]{1,0:T(8,128)S(1)}, f32[32,128]{1,0:T(8,128)S(1)}, u32[]{:S(2)}, u32[]{:S(2)}) collective-permute-start(f32[32,128]{1,0:T(8,128)S(1)} %get-tuple-element.30), channel_id=1, source_target_pairs={{0,3},{1,2},{2,1},{3,0},{4,7},{5,6},{6,5},{7,4},{8,11},{9,10},{10,... | collective-permute-start | bytes 49160 | tf_op jit(solution)/shard_map/ppermute | solution.py:195
  20.7 0.9 %collective-permute-start.11 = (f32[32,128]{1,0:T(8,128)S(1)}, f32[32,128]{1,0:T(8,128)S(1)}, u32[]{:S(2)}, u32[]{:S(2)}) collective-permute-start(f32[32,128]{1,0:T(8,128)S(1)} %get-tuple-element.31), channel_id=1, source_target_pairs={{0,2},{1,3},{2,0},{3,1},{4,6},{5,7},{6,4},{7,5},{8,10},{9,11},{10,... | collective-permute-start | bytes 49160 | tf_op jit(solution)/shard_map/ppermute | solution.py:195
  21.6 1.8 %collective-permute-start.12 = (f32[32,128]{1,0:T(8,128)S(1)}, f32[32,128]{1,0:T(8,128)S(1)}, u32[]{:S(2)}, u32[]{:S(2)}) collective-permute-start(f32[32,128]{1,0:T(8,128)S(1)} %get-tuple-element.32), channel_id=1, source_target_pairs={{0,1},{1,0},{2,3},{3,2},{4,5},{5,4},{6,7},{7,6},{8,9},{9,8},{10,11... | collective-permute-start | bytes 49160 | tf_op jit(solution)/shard_map/ppermute | solution.py:195
  23.4 1.2 %collective-permute-done.10.refs_1_ = f32[32,128]{1,0:T(8,128)S(1)} collective-permute-done((f32[32,128]{1,0:T(8,128)S(1)}, f32[32,128]{1,0:T(8,128)S(1)}, u32[]{:S(2)}, u32[]{:S(2)}) %collective-permute-start.10) | collective-permute-done | bytes 16416 | tf_op jit(solution)/shard_map/ppermute | solution.py:195
  24.6 0.9 %collective-permute-done.11.refs_2_ = f32[32,128]{1,0:T(8,128)S(1)} collective-permute-done((f32[32,128]{1,0:T(8,128)S(1)}, f32[32,128]{1,0:T(8,128)S(1)}, u32[]{:S(2)}, u32[]{:S(2)}) %collective-permute-start.11) | collective-permute-done | bytes 16416 | tf_op jit(solution)/shard_map/ppermute | solution.py:195
  25.5 0.0 collective-permute-done.12.refs_3_
  25.5 0.7 %sum_divide.1 = f32[32,64]{1,0:T(8,128)} custom-call(f32[32,128]{1,0:T(8,128)S(1)} %get-tuple-element.29.refs_0_, f32[32,128]{1,0:T(8,128)S(1)} %collective-permute-done.10.refs_1_, f32[32,128]{1,0:T(8,128)S(1)} %collective-permute-done.11.refs_2_, f32[32,128]{1,0:T(8,128)S(1)} %collective-permute-done.12.refs_3_), custom_call_target="tpu_custom_call" | custom-call | bytes 65536 | tf_op jit(solution)/shard_map/sum_divide/pallas_call | solution.py:201
  (9 shorter events, 0.1 us)
Async XLA Ops:
  0.0 9.2 %collective-permute-start.1 = (f32[1,32,64]{2,1,0:T(8,128)}, f32[1,32,64]{2,1,0:T(8,128)S(1)}, u32[]{:S(2)}, u32[]{:S(2)}) collective-permute-start(f32[1,32,64]{2,1,0:T(8,128)} %bitcast.4), channel_id=1, source_target_pairs={{0,8},{4,12},{8,0},{12,4},{16,24},{20,28},{24,16},{28,20},{1,9},{5... | collective-permute-start | bytes 24584 | tf_op jit(solution)/shard_map/ppermute | solution.py:195
  2.9 8.4 %collective-permute-start = (f32[3,32,256]{2,1,0:T(8,128)}, f32[3,32,256]{2,1,0:T(8,128)S(1)}, u32[]{:S(2)}, u32[]{:S(2)}) collective-permute-start(f32[3,32,256]{2,1,0:T(8,128)} %refs_0_.3), channel_id=1, source_target_pairs={{0,2},{1,3},{2,0},{3,1},{4,6},{5,7},{6,4},{7,5},{8,10},{9,11},{10,... | collective-permute-start | bytes 294920 | tf_op jit(solution)/shard_map/ppermute | solution.py:195
  5.5 6.3 %collective-permute-start.3 = (f32[3,32,256]{2,1,0:T(8,128)}, f32[3,32,256]{2,1,0:T(8,128)S(1)}, u32[]{:S(2)}, u32[]{:S(2)}) collective-permute-start(f32[3,32,256]{2,1,0:T(8,128)} %refs_0_.3), channel_id=1, source_target_pairs={{0,1},{1,0},{2,3},{3,2},{4,5},{5,4},{6,7},{7,6},{8,9},{9,8},{10,11... | collective-permute-start | bytes 294920 | tf_op jit(solution)/shard_map/ppermute | solution.py:195
  7.1 6.4 %collective-permute-start.5 = (f32[3,32,256]{2,1,0:T(8,128)}, f32[3,32,256]{2,1,0:T(8,128)S(1)}, u32[]{:S(2)}, u32[]{:S(2)}) collective-permute-start(f32[3,32,256]{2,1,0:T(8,128)} %refs_0_.2), channel_id=1, source_target_pairs={{0,16},{4,20},{8,24},{12,28},{16,0},{20,4},{24,8},{28,12},{1,17},{... | collective-permute-start | bytes 294920 | tf_op jit(solution)/shard_map/ppermute | solution.py:195
  8.6 4.8 %collective-permute-start.4 = (f32[3,32,256]{2,1,0:T(8,128)}, f32[3,32,256]{2,1,0:T(8,128)S(1)}, u32[]{:S(2)}, u32[]{:S(2)}) collective-permute-start(f32[3,32,256]{2,1,0:T(8,128)} %refs_0_.2), channel_id=1, source_target_pairs={{0,8},{4,12},{8,0},{12,4},{16,24},{20,28},{24,16},{28,20},{1,9},{5... | collective-permute-start | bytes 294920 | tf_op jit(solution)/shard_map/ppermute | solution.py:195
  9.2 5.7 %collective-permute-start.6 = (f32[3,32,256]{2,1,0:T(8,128)}, f32[3,32,256]{2,1,0:T(8,128)S(1)}, u32[]{:S(2)}, u32[]{:S(2)}) collective-permute-start(f32[3,32,256]{2,1,0:T(8,128)} %refs_0_.2), channel_id=1, source_target_pairs={{0,24},{4,28},{8,16},{12,20},{16,8},{20,12},{24,0},{28,4},{1,25},{... | collective-permute-start | bytes 294920 | tf_op jit(solution)/shard_map/ppermute | solution.py:195
  10.6 0.7 %copy-start.2 = (f32[64,32]{0,1:T(8,128)S(1)}, f32[64,32]{0,1:T(8,128)}, u32[]{:S(2)}) copy-start(f32[64,32]{0,1:T(8,128)} %param.5) | copy-start | bytes 24580
  11.3 3.6 %copy-start = (f32[3,32,256]{2,1,0:T(8,128)S(1)}, f32[3,32,256]{2,1,0:T(8,128)}, u32[]{:S(2)}) copy-start(f32[3,32,256]{2,1,0:T(8,128)} %refs_0_.2) | copy-start | bytes 294916
  11.3 5.3 %collective-permute-start.2 = (f32[3,32,256]{2,1,0:T(8,128)S(1)}, f32[3,32,256]{2,1,0:T(8,128)S(1)}, u32[]{:S(2)}, u32[]{:S(2)}) collective-permute-start(f32[3,32,256]{2,1,0:T(8,128)S(1)} %get-tuple-element.19.refs_4_.refs_1_), channel_id=1, source_target_pairs={{0,1},{1,0},{2,3},{3,2},{4,5},{5,4},{6,7},{7,6},{8,9},{9,8},{10,11... | collective-permute-start | bytes 294920 | tf_op jit(solution)/shard_map/ppermute | solution.py:195
  11.9 3.1 %copy-start.1 = (f32[3,32,256]{2,1,0:T(8,128)S(1)}, f32[3,32,256]{2,1,0:T(8,128)}, u32[]{:S(2)}) copy-start(f32[3,32,256]{2,1,0:T(8,128)} %refs_0_.3) | copy-start | bytes 294916
  11.9 4.2 %collective-permute-start.7 = (f32[2,32,64]{2,1,0:T(8,128)S(1)}, f32[2,32,64]{2,1,0:T(8,128)S(1)}, u32[]{:S(2)}, u32[]{:S(2)}) collective-permute-start(f32[2,32,64]{2,1,0:T(8,128)S(1)} %vectors.4.first_ref), channel_id=1, source_target_pairs={{0,16},{4,20},{8,24},{12,28},{16,0},{20,4},{24,8},{28,12},{1,17},{... | collective-permute-start | bytes 49160 | tf_op jit(solution)/shard_map/ppermute | solution.py:195
  14.9 2.7 %collective-permute-start.8 = (f32[4,3,32,256]{3,2,1,0:T(8,128)S(1)}, f32[4,3,32,256]{3,2,1,0:T(8,128)S(1)}, u32[]{:S(2)}, u32[]{:S(2)}) collective-permute-start(f32[4,3,32,256]{3,2,1,0:T(8,128)S(1)} %columns.1.refs_3_), channel_id=1, source_target_pairs={{0,4},{4,0},{8,12},{12,8},{16,20},{20,16},{24,28},{28,24},{1,5},{5... | collective-permute-start | bytes 1179656 | tf_op jit(solution)/shard_map/ppermute | solution.py:195
  16.1 1.5 %collective-permute-start.9 = (f32[4,32,64]{2,1,0:T(8,128)S(1)}, f32[4,32,64]{2,1,0:T(8,128)S(1)}, u32[]{:S(2)}, u32[]{:S(2)}) collective-permute-start(f32[4,32,64]{2,1,0:T(8,128)S(1)} %vectors.5.vecs_ref), channel_id=1, source_target_pairs={{0,4},{4,0},{8,12},{12,8},{16,20},{20,16},{24,28},{28,24},{1,5},{5... | collective-permute-start | bytes 98312 | tf_op jit(solution)/shard_map/ppermute | solution.py:195
  19.0 5.6 %collective-permute-start.10 = (f32[32,128]{1,0:T(8,128)S(1)}, f32[32,128]{1,0:T(8,128)S(1)}, u32[]{:S(2)}, u32[]{:S(2)}) collective-permute-start(f32[32,128]{1,0:T(8,128)S(1)} %get-tuple-element.30), channel_id=1, source_target_pairs={{0,3},{1,2},{2,1},{3,0},{4,7},{5,6},{6,5},{7,4},{8,11},{9,10},{10,... | collective-permute-start | bytes 49160 | tf_op jit(solution)/shard_map/ppermute | solution.py:195
  20.7 4.7 %collective-permute-start.11 = (f32[32,128]{1,0:T(8,128)S(1)}, f32[32,128]{1,0:T(8,128)S(1)}, u32[]{:S(2)}, u32[]{:S(2)}) collective-permute-start(f32[32,128]{1,0:T(8,128)S(1)} %get-tuple-element.31), channel_id=1, source_target_pairs={{0,2},{1,3},{2,0},{3,1},{4,6},{5,7},{6,4},{7,5},{8,10},{9,11},{10,... | collective-permute-start | bytes 49160 | tf_op jit(solution)/shard_map/ppermute | solution.py:195
  21.6 3.9 %collective-permute-start.12 = (f32[32,128]{1,0:T(8,128)S(1)}, f32[32,128]{1,0:T(8,128)S(1)}, u32[]{:S(2)}, u32[]{:S(2)}) collective-permute-start(f32[32,128]{1,0:T(8,128)S(1)} %get-tuple-element.32), channel_id=1, source_target_pairs={{0,1},{1,0},{2,3},{3,2},{4,5},{5,4},{6,7},{7,6},{8,9},{9,8},{10,11... | collective-permute-start | bytes 49160 | tf_op jit(solution)/shard_map/ppermute | solution.py:195

commit v3 on v2

--- a/solution.py
+++ b/solution.py
@@ -28,19 +28,19 @@
     out_ref[...] = in_ref[...]
 
 
-def join_kernel(first_ref, second_ref, out_ref):
-    count = second_ref.shape[0]
-    out_ref[0:count] = first_ref[...]
-    out_ref[count:] = second_ref[...]
-
-
-def after_far_kernel(far_ref, vec_ref, got_ref, far_out, vec_out):
-    far_out[...] = far_ref[...]
-    join_kernel(vec_ref, got_ref, vec_out)
-
-
-def pass_kernel(in_ref, *refs):
-    refs[-1][...] = in_ref[...]
+def pack_kernel(cols_ref, vec_ref, out_ref):
+    comps, frames, atoms = cols_ref.shape
+    for comp in range(comps):
+        out_ref[comp * frames:(comp + 1) * frames, :] = cols_ref[comp]
+    groups = atoms // vec_ref.shape[1]
+    step = frames // groups
+    out_ref[comps * frames:, :] = jnp.concatenate(
+        [vec_ref[group * step:(group + 1) * step, :] for group in range(groups)], axis=1
+    )
+
+
+def copy_kernel(in_ref, out_ref):
+    out_ref[...] = in_ref[...]
 
 
 def columns_kernel(n_blocks, *refs):
@@ -95,10 +95,11 @@
     return jnp.exp(-squared / BAND)
 
 
-def column_side(blocks_ref):
-    count, _, _, atoms = blocks_ref.shape
+def column_side(blocks_ref, frames):
+    count, _, atoms = blocks_ref.shape
     cols = [
-        centre(jnp.concatenate([blocks_ref[at, comp] for at in range(count)], axis=0)) for comp in range(3)
+        centre(jnp.concatenate([blocks_ref[at, comp * frames:(comp + 1) * frames, :] for at in range(count)], axis=0))
+        for comp in range(3)
     ]
     col_square = cols[0] * cols[0] + cols[1] * cols[1] + cols[2] * cols[2]
     norm = lax.dot_general(
@@ -109,11 +110,20 @@
     return jnp.concatenate([high, high, low], axis=1), norm
 
 
-def vector_side(vecs_ref):
-    count, frames, nv = vecs_ref.shape
-    ones = jnp.where(lax.broadcasted_iota(jnp.int32, (count * frames, LANES - nv), 1) == 0, 1.0, 0.0)
-    vecs = jnp.concatenate([vecs_ref[at] for at in range(count)], axis=0)
-    high, low = split(jnp.concatenate([vecs, ones], axis=1))
+def vector_side(blocks_ref, frames, nv):
+    count, _, atoms = blocks_ref.shape
+    groups = atoms // nv
+    step = frames // groups
+    lane = lax.broadcasted_iota(jnp.int32, (step, LANES), 1)
+    parts = []
+    for at in range(count):
+        for group in range(groups):
+            place = group * nv
+            piece = blocks_ref[at, 3 * frames:, place // LANES * LANES:place // LANES * LANES + LANES]
+            if place % LANES:
+                piece = pltpu.roll(piece, LANES - place % LANES, 1)
+            parts.append(jnp.where(lane < nv, piece, jnp.where(lane == nv, 1.0, 0.0)))
+    high, low = split(jnp.concatenate(parts, axis=0))
     return [high, high, low]
 
 
@@ -143,7 +153,7 @@
     rows_ref, row_norm_ref, tile_ref, side_ref, norm_ref, moment = refs[n_early + 1:]
     frames = slots[0].shape[1]
     groups, count, _ = tile_ref.shape
-    side, norm = column_side(blocks_ref)
+    side, norm = column_side(blocks_ref, frames)
     side_ref[...] = side
     norm_ref[...] = norm
     for group in range(groups):
@@ -167,11 +177,11 @@
     kernel_tile(rows, row_norm, side_ref[...], norm_ref[...], moment, tile_ref.at[groups - 1, count - frames:count])
 
 
-def second_kernel(frames, rows_ref, row_norm_ref, tile_ref, vecs_ref, blocks_ref, other_vecs_ref, *refs):
+def second_kernel(frames, nv, rows_ref, row_norm_ref, tile_ref, own_ref, blocks_ref, *refs):
     out_refs, moment, other_tile = refs[:-2], refs[-2], refs[-1]
     groups, count, _ = tile_ref.shape
-    side, norm = column_side(blocks_ref)
-    vecs = jnp.concatenate(vector_side(vecs_ref) + vector_side(other_vecs_ref), axis=0)
+    side, norm = column_side(blocks_ref, frames)
+    vecs = jnp.concatenate(vector_side(own_ref, frames, nv) + vector_side(blocks_ref, frames, nv), axis=0)
     for group in range(groups):
         kernel_tile(rows_ref[group], row_norm_ref[group], side, norm, moment, other_tile)
         high, low = split(tile_ref[group])
@@ -218,34 +228,26 @@
     row_masks = [n_col >> at for at in range(1, n_col.bit_length())]
     col_masks = [1 << at for at in range(1, n_row.bit_length() - 1)]
 
-    vecs = vectors.T[None]
-    got_vecs = exchange(vecs, "row", col_masks[0], n_row)
-    (vecs,) = call(copy_kernel, [((1, frames, nv), f32)], [vecs], "vectors", flops=1 << 30)
+    packed_shape = (comps * frames + frames * nv // atoms, atoms)
+    (packed,) = call(pack_kernel, [(packed_shape, f32)], [col_frames, vectors.T], "pack")
     order = [0]
     rows = {0: row_frames}
     for mask in row_masks:
         for slot in list(order):
             got = exchange(rows[slot], "col", mask, n_col)
             if not slot and mask == row_masks[0]:
-                got, vecs = call(
-                    after_far_kernel, [(got.shape, f32), ((2, frames, nv), f32)], [got, vecs, got_vecs], "after_far"
-                )
+                (got,) = call(copy_kernel, [(got.shape, f32)], [got], "far_rows", flops=10 << 30)
             rows[slot ^ mask] = got
             order.append(slot ^ mask)
     col_order = [0]
     for mask in col_masks:
         col_order = col_order + [slot ^ mask for slot in col_order]
-    cols = [col_frames] + [exchange(col_frames, "row", mask, n_row) for mask in col_order[1:]]
-    (vecs,) = call(pass_kernel, [((2, frames, nv), f32)], [vecs, rows[row_masks[1]]], "vectors")
-    for mask in col_masks[1:]:
-        got = exchange(vecs, "row", mask, n_row)
-        (vecs,) = call(join_kernel, [((2 * vecs.shape[0], frames, nv), f32)], [vecs, got], "vectors")
+    cols = [packed] + [exchange(packed, "row", mask, n_row) for mask in col_order[1:]]
     (blocks,) = call(
-        functools.partial(columns_kernel, len(cols)), [((len(cols), *col_frames.shape), f32)],
+        functools.partial(columns_kernel, len(cols)), [((len(cols), *packed_shape), f32)],
         [*cols, rows[row_masks[0]], rows[row_masks[1]]], "columns", flops=10 << 30,
     )
     other = exchange(blocks, "row", 1, n_row)
-    other_vecs = exchange(vecs, "row", 1, n_row)
 
     half_cols = n_row // 2 * frames
     count = min(n_col, max(1, LANES // frames)) * frames
@@ -266,8 +268,8 @@
         [pltpu.VMEM((3 * frames, 3 * half_cols), f32)], 32, work << 8, {3: 0, 4: 1, 5: 2},
     )
     parts = call(
-        functools.partial(second_kernel, frames), [((frames, LANES), f32)] * n_col,
-        [*kept, vecs, other, other_vecs], "second_tile", [moment, tile], 32, work,
+        functools.partial(second_kernel, frames, nv), [((frames, LANES), f32)] * n_col,
+        [*kept, blocks, other], "second_tile", [moment, tile], 32, work,
     )
     shares = [parts[0]] + [
         exchange(parts[order.index(mask)], "col", mask, n_col) for mask in range(n_col - 1, 0, -1)

time: 26.5 us -> 25.4 us (0.958)
  starting transfers between devices: 17.8 us -> 14.2 us
  waiting for transfers between devices: 3.94 us -> 5.56 us
  local copies, waits for them, and re-layouts: 0.73 us -> 1.61 us
    ppermute x13 -> x10, starting transfers between devices: 17.8 us -> 14.2 us  [exchange(): return lax.ppermute(x, axis, [(at, at ^ mask) for at in range(count)])]
    ppermute x13 -> x10, waiting for transfers between devices: 3.94 us -> 5.56 us  [exchange(): return lax.ppermute(x, axis, [(at, at ^ mask) for at in range(count)])]
    unnamed x6, local copies, waits for them, and re-layouts: 0.73 us -> 1.61 us
    pallas_call x9 -> x7, Pallas kernels: 3.7 us -> 3.76 us  [call(): pl.pallas_call(kernel, out_shape=out_shape, in_specs=[VM] * len(ins), out...]
  transfers between devices with their start and end apart: 13 -> 10, of which waited for: 4 -> 6; matrix products, arithmetic and copies ran while one was open for 0% -> 0% of each run, Pallas kernels for 6% -> 7%
where the time goes in v3:
time: 25.4 us; the launch traced here: 25.1 us
  starting transfers between devices  14.2 us (56%)
  waiting for transfers between devices  5.56 us (22%)
  Pallas kernels  3.76 us (15%)
  local copies, waits for them, and re-layouts  1.61 us (6%)
    ppermute x10, starting transfers between devices, exchange(): return lax.ppermute(x, axis, [(at, at ^ mask) for at in range(count)])  14.2 us
    ppermute x10, waiting for transfers between devices, exchange(): return lax.ppermute(x, axis, [(at, at ^ mask) for at in range(count)])  5.56 us
    pallas_call x7, Pallas kernels, call(): pl.pallas_call(kernel, out_shape=out_shape, in_specs=[VM] * len(ins), out...  3.76 us
    unnamed x6, local copies, waits for them, and re-layouts  1.61 us
  transfers between devices with their start and end apart: 10, of which 6 were waited for; matrix products, arithmetic and copies ran while one was open for 0% of the time, Pallas kernels for 7%

profile of v3, /device:TPU:0, one launch (start us, length us, event | category | flops | bytes accessed | tf_op | source)
XLA Modules:
  0.0 25.1 jit_solution(3411026394078736744)
XLA Ops:
  0.0 4.0 %collective-permute-start = (f32[3,32,256]{2,1,0:T(8,128)}, f32[3,32,256]{2,1,0:T(8,128)S(1)}, u32[]{:S(2)}, u32[]{:S(2)}) collective-permute-start(f32[3,32,256]{2,1,0:T(8,128)} %refs_0_.1), channel_id=1, source_target_pairs={{0,2},{1,3},{2,0},{3,1},{4,6},{5,7},{6,4},{7,5},{8,10},{9,11},{10,... | collective-permute-start | bytes 294920 | tf_op jit(solution)/shard_map/ppermute | solution.py:205
  4.0 0.0 copy-start
  4.0 0.9 %copy-done = f32[3,32,256]{2,1,0:T(8,128)S(1)} copy-done((f32[3,32,256]{2,1,0:T(8,128)S(1)}, f32[3,32,256]{2,1,0:T(8,128)}, u32[]{:S(2)}) %copy-start) | copy-done | bytes 98328
  4.9 0.0 copy-start.1
  4.9 0.7 %copy-done.1 = f32[64,32]{0,1:T(8,128)S(1)} copy-done((f32[64,32]{0,1:T(8,128)S(1)}, f32[64,32]{0,1:T(8,128)}, u32[]{:S(2)}) %copy-start.1) | copy-done | bytes 8216
  5.6 0.0 copy-start.2
  5.7 0.1 pack.1.refs_0_
  5.7 1.5 %collective-permute-start.3 = (f32[104,256]{1,0:T(8,128)S(1)}, f32[104,256]{1,0:T(8,128)S(1)}, u32[]{:S(2)}, u32[]{:S(2)}) collective-permute-start(f32[104,256]{1,0:T(8,128)S(1)} %pack.1.refs_0_), channel_id=1, source_target_pairs={{0,8},{4,12},{8,0},{12,4},{16,24},{20,28},{24,16},{28,20},{1,9},{5... | collective-permute-start | bytes 319496 | tf_op jit(solution)/shard_map/ppermute | solution.py:205
  7.2 1.5 %collective-permute-start.4 = (f32[104,256]{1,0:T(8,128)S(1)}, f32[104,256]{1,0:T(8,128)S(1)}, u32[]{:S(2)}, u32[]{:S(2)}) collective-permute-start(f32[104,256]{1,0:T(8,128)S(1)} %pack.1.refs_0_), channel_id=1, source_target_pairs={{0,16},{4,20},{8,24},{12,28},{16,0},{20,4},{24,8},{28,12},{1,17},{... | collective-permute-start | bytes 319496 | tf_op jit(solution)/shard_map/ppermute | solution.py:205
  8.7 0.5 %collective-permute-start.5 = (f32[104,256]{1,0:T(8,128)S(1)}, f32[104,256]{1,0:T(8,128)S(1)}, u32[]{:S(2)}, u32[]{:S(2)}) collective-permute-start(f32[104,256]{1,0:T(8,128)S(1)} %pack.1.refs_0_), channel_id=1, source_target_pairs={{0,24},{4,28},{8,16},{12,20},{16,8},{20,12},{24,0},{28,4},{1,25},{... | collective-permute-start | bytes 319496 | tf_op jit(solution)/shard_map/ppermute | solution.py:205
  9.2 0.0 copy-done.2
  9.2 1.6 %collective-permute-start.2 = (f32[3,32,256]{2,1,0:T(8,128)S(1)}, f32[3,32,256]{2,1,0:T(8,128)S(1)}, u32[]{:S(2)}, u32[]{:S(2)}) collective-permute-start(f32[3,32,256]{2,1,0:T(8,128)S(1)} %copy-done.2), channel_id=1, source_target_pairs={{0,1},{1,0},{2,3},{3,2},{4,5},{5,4},{6,7},{7,6},{8,9},{9,8},{10,11... | collective-permute-start | bytes 294920 | tf_op jit(solution)/shard_map/ppermute | solution.py:205
  10.8 0.0 collective-permute-done.in_ref
  10.8 0.5 %collective-permute-start.1 = (f32[3,32,256]{2,1,0:T(8,128)S(1)}, f32[3,32,256]{2,1,0:T(8,128)S(1)}, u32[]{:S(2)}, u32[]{:S(2)}) collective-permute-start(f32[3,32,256]{2,1,0:T(8,128)S(1)} %far_rows.1.refs_4_.refs_1_), channel_id=1, source_target_pairs={{0,1},{1,0},{2,3},{3,2},{4,5},{5,4},{6,7},{7,6},{8,9},{9,8},{10,11... | collective-permute-start | bytes 294920 | tf_op jit(solution)/shard_map/ppermute | solution.py:205
  11.3 2.7 %collective-permute-done.2.refs_5_.refs_2_ = f32[3,32,256]{2,1,0:T(8,128)S(1)} collective-permute-done((f32[3,32,256]{2,1,0:T(8,128)S(1)}, f32[3,32,256]{2,1,0:T(8,128)S(1)}, u32[]{:S(2)}, u32[]{:S(2)}) %collective-permute-start.2) | collective-permute-done | bytes 98336 | tf_op jit(solution)/shard_map/ppermute | solution.py:205
  14.0 0.0 collective-permute-done.3.refs_1_
  14.0 0.0 collective-permute-done.4.refs_2_
  14.0 0.3 %collective-permute-done.5.refs_3_ = f32[104,256]{1,0:T(8,128)S(1)} collective-permute-done((f32[104,256]{1,0:T(8,128)S(1)}, f32[104,256]{1,0:T(8,128)S(1)}, u32[]{:S(2)}, u32[]{:S(2)}) %collective-permute-start.5) | collective-permute-done | bytes 106528 | tf_op jit(solution)/shard_map/ppermute | solution.py:205
  14.4 0.1 collective-permute-start.6
  14.5 1.1 %early_tile.1 = (bf16[1,384,768]{2,1,0:T(8,128)(2,1)S(1)}, f32[1,128,128]{2,1,0:T(8,128)S(1)}, f32[1,128,128]{2,1,0:T(8,128)S(1)}, bf16[384,768]{1,0:T(8,128)(2,1)S(1)}, f32[8,128]{1,0:T(8,128)S(1)}) custom-call(f32[3,32,256]{2,1,0:T(8,128)S(1)} %copy-done.2, f32[3,32,256]{2,1,0:T(8,128)S(1)} %far_rows.1.refs_4_.refs_1_, ...), custom_call_target="tpu_custom_call" | custom-call | flops 226492416 | bytes 720896 | tf_op jit(solution)/shard_map/early_tile/pallas_call | solution.py:211
  15.5 0.0 collective-permute-done.1.row_ref
  15.6 0.5 %last_tile.1 = (bf16[1,384,768]{2,1,0:T(8,128)(2,1)S(1)}, f32[1,128,128]{2,1,0:T(8,128)S(1)}, f32[1,128,128]{2,1,0:T(8,128)S(1)}) custom-call(f32[3,32,256]{2,1,0:T(8,128)S(1)} %collective-permute-done.1.row_ref, bf16[384,768]{1,0:T(8,128)(2,1)S(1)} %get-tuple-element.17.side_ref, ...), custom_call_target="tpu_custom_call", output_to_operand_aliasing={{0}: (3, {}), {1}: (4, {}), {2}: (5, {})} | custom-call | flops 57982058496 | bytes 2592768 | tf_op jit(solution)/shard_map/last_tile/pallas_call | solution.py:211
  16.1 0.1 collective-permute-done.6.blocks_ref
  16.2 1.4 %second_tile.1 = (f32[32,128]{1,0:T(8,128)S(1)}, f32[32,128]{1,0:T(8,128)S(1)}, f32[32,128]{1,0:T(8,128)S(1)}, f32[32,128]{1,0:T(8,128)S(1)}) custom-call(bf16[1,384,768]{2,1,0:T(8,128)(2,1)S(1)} %get-tuple-element.22.rows_ref, f32[1,128,128]{2,1,0:T(8,128)S(1)} %get-tuple-element.23.row_norm_ref, f32[1,128,128]{2,1,0:T(8,128)S(1)} %get-tuple-element.24.tile_ref, ...), custom_call_target="tpu_custom_call" | custom-call | flops 226492416 | bytes 2162688 | tf_op jit(solution)/shard_map/second_tile/pallas_call | solution.py:211
  17.6 1.9 %collective-permute-start.7 = (f32[32,128]{1,0:T(8,128)S(1)}, f32[32,128]{1,0:T(8,128)S(1)}, u32[]{:S(2)}, u32[]{:S(2)}) collective-permute-start(f32[32,128]{1,0:T(8,128)S(1)} %get-tuple-element.26), channel_id=1, source_target_pairs={{0,3},{1,2},{2,1},{3,0},{4,7},{5,6},{6,5},{7,4},{8,11},{9,10},{10,... | collective-permute-start | bytes 49160 | tf_op jit(solution)/shard_map/ppermute | solution.py:205
  19.4 1.3 %collective-permute-start.8 = (f32[32,128]{1,0:T(8,128)S(1)}, f32[32,128]{1,0:T(8,128)S(1)}, u32[]{:S(2)}, u32[]{:S(2)}) collective-permute-start(f32[32,128]{1,0:T(8,128)S(1)} %get-tuple-element.27), channel_id=1, source_target_pairs={{0,2},{1,3},{2,0},{3,1},{4,6},{5,7},{6,4},{7,5},{8,10},{9,11},{10,... | collective-permute-start | bytes 49160 | tf_op jit(solution)/shard_map/ppermute | solution.py:205
  20.7 1.3 %collective-permute-start.9 = (f32[32,128]{1,0:T(8,128)S(1)}, f32[32,128]{1,0:T(8,128)S(1)}, u32[]{:S(2)}, u32[]{:S(2)}) collective-permute-start(f32[32,128]{1,0:T(8,128)S(1)} %get-tuple-element.28), channel_id=1, source_target_pairs={{0,1},{1,0},{2,3},{3,2},{4,5},{5,4},{6,7},{7,6},{8,9},{9,8},{10,11... | collective-permute-start | bytes 49160 | tf_op jit(solution)/shard_map/ppermute | solution.py:205
  22.1 1.2 %collective-permute-done.7.refs_1_ = f32[32,128]{1,0:T(8,128)S(1)} collective-permute-done((f32[32,128]{1,0:T(8,128)S(1)}, f32[32,128]{1,0:T(8,128)S(1)}, u32[]{:S(2)}, u32[]{:S(2)}) %collective-permute-start.7) | collective-permute-done | bytes 16416 | tf_op jit(solution)/shard_map/ppermute | solution.py:205
  23.2 0.9 %collective-permute-done.8.refs_2_ = f32[32,128]{1,0:T(8,128)S(1)} collective-permute-done((f32[32,128]{1,0:T(8,128)S(1)}, f32[32,128]{1,0:T(8,128)S(1)}, u32[]{:S(2)}, u32[]{:S(2)}) %collective-permute-start.8) | collective-permute-done | bytes 16416 | tf_op jit(solution)/shard_map/ppermute | solution.py:205
  24.1 0.4 %collective-permute-done.9.refs_3_ = f32[32,128]{1,0:T(8,128)S(1)} collective-permute-done((f32[32,128]{1,0:T(8,128)S(1)}, f32[32,128]{1,0:T(8,128)S(1)}, u32[]{:S(2)}, u32[]{:S(2)}) %collective-permute-start.9) | collective-permute-done | bytes 16416 | tf_op jit(solution)/shard_map/ppermute | solution.py:205
  24.5 0.7 %sum_divide.1 = f32[32,64]{1,0:T(8,128)} custom-call(f32[32,128]{1,0:T(8,128)S(1)} %get-tuple-element.25.refs_0_, f32[32,128]{1,0:T(8,128)S(1)} %collective-permute-done.7.refs_1_, f32[32,128]{1,0:T(8,128)S(1)} %collective-permute-done.8.refs_2_, f32[32,128]{1,0:T(8,128)S(1)} %collective-permute-done.9.refs_3_), custom_call_target="tpu_custom_call" | custom-call | bytes 65536 | tf_op jit(solution)/shard_map/sum_divide/pallas_call | solution.py:211
  (2 shorter events, 0.0 us)
Async XLA Ops:
  0.0 10.8 %collective-permute-start = (f32[3,32,256]{2,1,0:T(8,128)}, f32[3,32,256]{2,1,0:T(8,128)S(1)}, u32[]{:S(2)}, u32[]{:S(2)}) collective-permute-start(f32[3,32,256]{2,1,0:T(8,128)} %refs_0_.1), channel_id=1, source_target_pairs={{0,2},{1,3},{2,0},{3,1},{4,6},{5,7},{6,4},{7,5},{8,10},{9,11},{10,... | collective-permute-start | bytes 294920 | tf_op jit(solution)/shard_map/ppermute | solution.py:205
  4.0 0.9 %copy-start = (f32[3,32,256]{2,1,0:T(8,128)S(1)}, f32[3,32,256]{2,1,0:T(8,128)}, u32[]{:S(2)}) copy-start(f32[3,32,256]{2,1,0:T(8,128)} %cols_ref.1) | copy-start | bytes 294916
  4.9 0.7 %copy-start.1 = (f32[64,32]{0,1:T(8,128)S(1)}, f32[64,32]{0,1:T(8,128)}, u32[]{:S(2)}) copy-start(f32[64,32]{0,1:T(8,128)} %param.5) | copy-start | bytes 24580
  5.6 3.6 %copy-start.2 = (f32[3,32,256]{2,1,0:T(8,128)S(1)}, f32[3,32,256]{2,1,0:T(8,128)}, u32[]{:S(2)}) copy-start(f32[3,32,256]{2,1,0:T(8,128)} %refs_0_.1) | copy-start | bytes 294916
  5.7 8.3 %collective-permute-start.3 = (f32[104,256]{1,0:T(8,128)S(1)}, f32[104,256]{1,0:T(8,128)S(1)}, u32[]{:S(2)}, u32[]{:S(2)}) collective-permute-start(f32[104,256]{1,0:T(8,128)S(1)} %pack.1.refs_0_), channel_id=1, source_target_pairs={{0,8},{4,12},{8,0},{12,4},{16,24},{20,28},{24,16},{28,20},{1,9},{5... | collective-permute-start | bytes 319496 | tf_op jit(solution)/shard_map/ppermute | solution.py:205
  7.2 6.8 %collective-permute-start.4 = (f32[104,256]{1,0:T(8,128)S(1)}, f32[104,256]{1,0:T(8,128)S(1)}, u32[]{:S(2)}, u32[]{:S(2)}) collective-permute-start(f32[104,256]{1,0:T(8,128)S(1)} %pack.1.refs_0_), channel_id=1, source_target_pairs={{0,16},{4,20},{8,24},{12,28},{16,0},{20,4},{24,8},{28,12},{1,17},{... | collective-permute-start | bytes 319496 | tf_op jit(solution)/shard_map/ppermute | solution.py:205
  8.7 5.6 %collective-permute-start.5 = (f32[104,256]{1,0:T(8,128)S(1)}, f32[104,256]{1,0:T(8,128)S(1)}, u32[]{:S(2)}, u32[]{:S(2)}) collective-permute-start(f32[104,256]{1,0:T(8,128)S(1)} %pack.1.refs_0_), channel_id=1, source_target_pairs={{0,24},{4,28},{8,16},{12,20},{16,8},{20,12},{24,0},{28,4},{1,25},{... | collective-permute-start | bytes 319496 | tf_op jit(solution)/shard_map/ppermute | solution.py:205
  9.2 4.8 %collective-permute-start.2 = (f32[3,32,256]{2,1,0:T(8,128)S(1)}, f32[3,32,256]{2,1,0:T(8,128)S(1)}, u32[]{:S(2)}, u32[]{:S(2)}) collective-permute-start(f32[3,32,256]{2,1,0:T(8,128)S(1)} %copy-done.2), channel_id=1, source_target_pairs={{0,1},{1,0},{2,3},{3,2},{4,5},{5,4},{6,7},{7,6},{8,9},{9,8},{10,11... | collective-permute-start | bytes 294920 | tf_op jit(solution)/shard_map/ppermute | solution.py:205
  10.8 4.7 %collective-permute-start.1 = (f32[3,32,256]{2,1,0:T(8,128)S(1)}, f32[3,32,256]{2,1,0:T(8,128)S(1)}, u32[]{:S(2)}, u32[]{:S(2)}) collective-permute-start(f32[3,32,256]{2,1,0:T(8,128)S(1)} %far_rows.1.refs_4_.refs_1_), channel_id=1, source_target_pairs={{0,1},{1,0},{2,3},{3,2},{4,5},{5,4},{6,7},{7,6},{8,9},{9,8},{10,11... | collective-permute-start | bytes 294920 | tf_op jit(solution)/shard_map/ppermute | solution.py:205
  14.4 1.8 %collective-permute-start.6 = (f32[4,104,256]{2,1,0:T(8,128)S(1)}, f32[4,104,256]{2,1,0:T(8,128)S(1)}, u32[]{:S(2)}, u32[]{:S(2)}) collective-permute-start(f32[4,104,256]{2,1,0:T(8,128)S(1)} %columns.1.refs_3_.own_ref), channel_id=1, source_target_pairs={{0,4},{4,0},{8,12},{12,8},{16,20},{20,16},{24,28},{28,24},{1,5},{5... | collective-permute-start | bytes 1277960 | tf_op jit(solution)/shard_map/ppermute | solution.py:205
  17.6 5.6 %collective-permute-start.7 = (f32[32,128]{1,0:T(8,128)S(1)}, f32[32,128]{1,0:T(8,128)S(1)}, u32[]{:S(2)}, u32[]{:S(2)}) collective-permute-start(f32[32,128]{1,0:T(8,128)S(1)} %get-tuple-element.26), channel_id=1, source_target_pairs={{0,3},{1,2},{2,1},{3,0},{4,7},{5,6},{6,5},{7,4},{8,11},{9,10},{10,... | collective-permute-start | bytes 49160 | tf_op jit(solution)/shard_map/ppermute | solution.py:205
  19.4 4.6 %collective-permute-start.8 = (f32[32,128]{1,0:T(8,128)S(1)}, f32[32,128]{1,0:T(8,128)S(1)}, u32[]{:S(2)}, u32[]{:S(2)}) collective-permute-start(f32[32,128]{1,0:T(8,128)S(1)} %get-tuple-element.27), channel_id=1, source_target_pairs={{0,2},{1,3},{2,0},{3,1},{4,6},{5,7},{6,4},{7,5},{8,10},{9,11},{10,... | collective-permute-start | bytes 49160 | tf_op jit(solution)/shard_map/ppermute | solution.py:205
  20.7 3.7 %collective-permute-start.9 = (f32[32,128]{1,0:T(8,128)S(1)}, f32[32,128]{1,0:T(8,128)S(1)}, u32[]{:S(2)}, u32[]{:S(2)}) collective-permute-start(f32[32,128]{1,0:T(8,128)S(1)} %get-tuple-element.28), channel_id=1, source_target_pairs={{0,1},{1,0},{2,3},{3,2},{4,5},{5,4},{6,7},{7,6},{8,9},{9,8},{10,11... | collective-permute-start | bytes 49160 | tf_op jit(solution)/shard_map/ppermute | solution.py:205

commit v4 on v3

--- a/solution.py
+++ b/solution.py
@@ -28,14 +28,13 @@
     out_ref[...] = in_ref[...]
 
 
-def pack_kernel(cols_ref, vec_ref, out_ref):
-    comps, frames, atoms = cols_ref.shape
-    for comp in range(comps):
-        out_ref[comp * frames:(comp + 1) * frames, :] = cols_ref[comp]
-    groups = atoms // vec_ref.shape[1]
+def pack_kernel(frames, nv, in_ref, out_ref):
+    used = in_ref.shape[0] - frames
+    groups = in_ref.shape[1] // nv
     step = frames // groups
-    out_ref[comps * frames:, :] = jnp.concatenate(
-        [vec_ref[group * step:(group + 1) * step, :] for group in range(groups)], axis=1
+    out_ref[0:used, :] = in_ref[0:used, :]
+    out_ref[used:, :] = jnp.concatenate(
+        [in_ref[used + group * step:used + (group + 1) * step, 0:nv] for group in range(groups)], axis=1
     )
 
 
@@ -229,7 +228,10 @@
     col_masks = [1 << at for at in range(1, n_row.bit_length() - 1)]
 
     packed_shape = (comps * frames + frames * nv // atoms, atoms)
-    (packed,) = call(pack_kernel, [(packed_shape, f32)], [col_frames, vectors.T], "pack")
+    both = jnp.concatenate(
+        [col_frames.reshape(comps * frames, atoms), jnp.pad(vectors.T, ((0, 0), (0, atoms - nv)))], axis=0
+    )
+    (packed,) = call(functools.partial(pack_kernel, frames, nv), [(packed_shape, f32)], [both], "pack")
     order = [0]
     rows = {0: row_frames}
     for mask in row_masks:
@@ -245,7 +247,7 @@
     cols = [packed] + [exchange(packed, "row", mask, n_row) for mask in col_order[1:]]
     (blocks,) = call(
         functools.partial(columns_kernel, len(cols)), [((len(cols), *packed_shape), f32)],
-        [*cols, rows[row_masks[0]], rows[row_masks[1]]], "columns", flops=10 << 30,
+        [*cols, rows[row_masks[0]]], "columns", flops=10 << 30,
     )
     other = exchange(blocks, "row", 1, n_row)
 

time: 25.4 us -> 25 us (0.984)
  local copies, waits for them, and re-layouts: 1.61 us -> 0.01 us
  other arithmetic: 0 us -> 0.92 us
  waiting for transfers between devices: 5.56 us -> 5.86 us
    unnamed x6 -> x2, local copies, waits for them, and re-layouts: 1.61 us -> 0.01 us
    concatenate x0 -> x1, other arithmetic: none -> 0.92 us  [per_device(): jnp.concatenate([col_frames.reshape(comps * frames, atoms), jnp.pad(vecto...]
    ppermute x10, waiting for transfers between devices: 5.56 us -> 5.86 us  [exchange(): return lax.ppermute(x, axis, [(at, at ^ mask) for at in range(count)])]
  transfers between devices with their start and end apart: 10 -> 10, of which waited for: 6 -> 5; matrix products, arithmetic and copies ran while one was open for 0% -> 4% of each run, Pallas kernels for 7% -> 7%
where the time goes in v4:
time: 25 us; the launch traced here: 24.8 us
  starting transfers between devices  14.2 us (57%)
  waiting for transfers between devices  5.86 us (23%)
  Pallas kernels  3.77 us (15%)
  other arithmetic  0.92 us (4%)
    ppermute x10, starting transfers between devices, exchange(): return lax.ppermute(x, axis, [(at, at ^ mask) for at in range(count)])  14.2 us
    ppermute x10, waiting for transfers between devices, exchange(): return lax.ppermute(x, axis, [(at, at ^ mask) for at in range(count)])  5.86 us
    pallas_call x7, Pallas kernels, call(): pl.pallas_call(kernel, out_shape=out_shape, in_specs=[VM] * len(ins), out...  3.77 us
    concatenate x1, other arithmetic, per_device(): jnp.concatenate([col_frames.reshape(comps * frames, atoms), jnp.pad(vecto...  0.92 us
  transfers between devices with their start and end apart: 10, of which 5 were waited for; matrix products, arithmetic and copies ran while one was open for 4% of the time, Pallas kernels for 7%

profile of v4, /device:TPU:0, one launch (start us, length us, event | category | flops | bytes accessed | tf_op | source)
XLA Modules:
  0.0 24.8 jit_solution(2606064803703569402)
XLA Ops:
  0.0 4.0 %collective-permute-start = (f32[3,32,256]{2,1,0:T(8,128)}, f32[3,32,256]{2,1,0:T(8,128)S(1)}, u32[]{:S(2)}, u32[]{:S(2)}) collective-permute-start(f32[3,32,256]{2,1,0:T(8,128)} %refs_0_.1), channel_id=1, source_target_pairs={{0,2},{1,3},{2,0},{3,1},{4,6},{5,7},{6,4},{7,5},{8,10},{9,11},{10,... | collective-permute-start | bytes 294920 | tf_op jit(solution)/shard_map/ppermute | solution.py:204
  4.0 0.9 %select_maximum_fusion.in_ref = f32[128,256]{1,0:T(8,128)S(1)} fusion(f32[32,64]{1,0:T(8,128)} %bitcast.4, f32[96,256]{1,0:T(8,128)} %bitcast.3), kind=kLoop, calls=%fused_computation | loop fusion | flops 98304 | bytes 237568 | tf_op jit(solution)/shard_map/concatenate | solution.py:231
  5.0 0.0 copy-start
  5.0 0.1 pack.1.refs_0_
  5.0 1.5 %collective-permute-start.3 = (f32[104,256]{1,0:T(8,128)S(1)}, f32[104,256]{1,0:T(8,128)S(1)}, u32[]{:S(2)}, u32[]{:S(2)}) collective-permute-start(f32[104,256]{1,0:T(8,128)S(1)} %pack.1.refs_0_), channel_id=1, source_target_pairs={{0,8},{4,12},{8,0},{12,4},{16,24},{20,28},{24,16},{28,20},{1,9},{5... | collective-permute-start | bytes 319496 | tf_op jit(solution)/shard_map/ppermute | solution.py:204
  6.5 1.5 %collective-permute-start.4 = (f32[104,256]{1,0:T(8,128)S(1)}, f32[104,256]{1,0:T(8,128)S(1)}, u32[]{:S(2)}, u32[]{:S(2)}) collective-permute-start(f32[104,256]{1,0:T(8,128)S(1)} %pack.1.refs_0_), channel_id=1, source_target_pairs={{0,16},{4,20},{8,24},{12,28},{16,0},{20,4},{24,8},{28,12},{1,17},{... | collective-permute-start | bytes 319496 | tf_op jit(solution)/shard_map/ppermute | solution.py:204
  8.1 0.5 %collective-permute-start.5 = (f32[104,256]{1,0:T(8,128)S(1)}, f32[104,256]{1,0:T(8,128)S(1)}, u32[]{:S(2)}, u32[]{:S(2)}) collective-permute-start(f32[104,256]{1,0:T(8,128)S(1)} %pack.1.refs_0_), channel_id=1, source_target_pairs={{0,24},{4,28},{8,16},{12,20},{16,8},{20,12},{24,0},{28,4},{1,25},{... | collective-permute-start | bytes 319496 | tf_op jit(solution)/shard_map/ppermute | solution.py:204
  8.5 0.0 copy-done
  8.6 1.6 %collective-permute-start.2 = (f32[3,32,256]{2,1,0:T(8,128)S(1)}, f32[3,32,256]{2,1,0:T(8,128)S(1)}, u32[]{:S(2)}, u32[]{:S(2)}) collective-permute-start(f32[3,32,256]{2,1,0:T(8,128)S(1)} %copy-done), channel_id=1, source_target_pairs={{0,1},{1,0},{2,3},{3,2},{4,5},{5,4},{6,7},{7,6},{8,9},{9,8},{10,11... | collective-permute-start | bytes 294920 | tf_op jit(solution)/shard_map/ppermute | solution.py:204
  10.1 0.0 collective-permute-done.in_ref
  10.1 0.5 %collective-permute-start.1 = (f32[3,32,256]{2,1,0:T(8,128)S(1)}, f32[3,32,256]{2,1,0:T(8,128)S(1)}, u32[]{:S(2)}, u32[]{:S(2)}) collective-permute-start(f32[3,32,256]{2,1,0:T(8,128)S(1)} %far_rows.1.refs_4_.refs_1_), channel_id=1, source_target_pairs={{0,1},{1,0},{2,3},{3,2},{4,5},{5,4},{6,7},{7,6},{8,9},{9,8},{10,11... | collective-permute-start | bytes 294920 | tf_op jit(solution)/shard_map/ppermute | solution.py:204
  10.7 0.0 collective-permute-done.3.refs_1_
  10.7 1.7 %collective-permute-done.4.refs_2_ = f32[104,256]{1,0:T(8,128)S(1)} collective-permute-done((f32[104,256]{1,0:T(8,128)S(1)}, f32[104,256]{1,0:T(8,128)S(1)}, u32[]{:S(2)}, u32[]{:S(2)}) %collective-permute-start.4) | collective-permute-done | bytes 106528 | tf_op jit(solution)/shard_map/ppermute | solution.py:204
  12.4 1.3 %collective-permute-done.5.refs_3_ = f32[104,256]{1,0:T(8,128)S(1)} collective-permute-done((f32[104,256]{1,0:T(8,128)S(1)}, f32[104,256]{1,0:T(8,128)S(1)}, u32[]{:S(2)}, u32[]{:S(2)}) %collective-permute-start.5) | collective-permute-done | bytes 106528 | tf_op jit(solution)/shard_map/ppermute | solution.py:204
  13.7 0.1 collective-permute-start.6
  13.8 0.0 collective-permute-done.2.refs_2_
  13.8 1.1 %early_tile.1 = (bf16[1,384,768]{2,1,0:T(8,128)(2,1)S(1)}, f32[1,128,128]{2,1,0:T(8,128)S(1)}, f32[1,128,128]{2,1,0:T(8,128)S(1)}, bf16[384,768]{1,0:T(8,128)(2,1)S(1)}, f32[8,128]{1,0:T(8,128)S(1)}) custom-call(f32[3,32,256]{2,1,0:T(8,128)S(1)} %copy-done, f32[3,32,256]{2,1,0:T(8,128)S(1)} %far_rows.1.refs_4_.refs_1_, ...), custom_call_target="tpu_custom_call" | custom-call | flops 226492416 | bytes 720896 | tf_op jit(solution)/shard_map/early_tile/pallas_call | solution.py:210
  14.9 0.0 collective-permute-done.1.row_ref
  14.9 0.5 %last_tile.1 = (bf16[1,384,768]{2,1,0:T(8,128)(2,1)S(1)}, f32[1,128,128]{2,1,0:T(8,128)S(1)}, f32[1,128,128]{2,1,0:T(8,128)S(1)}) custom-call(f32[3,32,256]{2,1,0:T(8,128)S(1)} %collective-permute-done.1.row_ref, bf16[384,768]{1,0:T(8,128)(2,1)S(1)} %get-tuple-element.17.side_ref, ...), custom_call_target="tpu_custom_call", output_to_operand_aliasing={{0}: (3, {}), {1}: (4, {}), {2}: (5, {})} | custom-call | flops 57982058496 | bytes 2592768 | tf_op jit(solution)/shard_map/last_tile/pallas_call | solution.py:210
  15.4 0.1 collective-permute-done.6.blocks_ref
  15.5 1.4 %second_tile.1 = (f32[32,128]{1,0:T(8,128)S(1)}, f32[32,128]{1,0:T(8,128)S(1)}, f32[32,128]{1,0:T(8,128)S(1)}, f32[32,128]{1,0:T(8,128)S(1)}) custom-call(bf16[1,384,768]{2,1,0:T(8,128)(2,1)S(1)} %get-tuple-element.22.rows_ref, f32[1,128,128]{2,1,0:T(8,128)S(1)} %get-tuple-element.23.row_norm_ref, f32[1,128,128]{2,1,0:T(8,128)S(1)} %get-tuple-element.24.tile_ref, ...), custom_call_target="tpu_custom_call" | custom-call | flops 226492416 | bytes 2162688 | tf_op jit(solution)/shard_map/second_tile/pallas_call | solution.py:210
  16.9 2.5 %collective-permute-start.7 = (f32[32,128]{1,0:T(8,128)S(1)}, f32[32,128]{1,0:T(8,128)S(1)}, u32[]{:S(2)}, u32[]{:S(2)}) collective-permute-start(f32[32,128]{1,0:T(8,128)S(1)} %get-tuple-element.26), channel_id=1, source_target_pairs={{0,3},{1,2},{2,1},{3,0},{4,7},{5,6},{6,5},{7,4},{8,11},{9,10},{10,... | collective-permute-start | bytes 49160 | tf_op jit(solution)/shard_map/ppermute | solution.py:204
  19.5 0.6 %collective-permute-start.8 = (f32[32,128]{1,0:T(8,128)S(1)}, f32[32,128]{1,0:T(8,128)S(1)}, u32[]{:S(2)}, u32[]{:S(2)}) collective-permute-start(f32[32,128]{1,0:T(8,128)S(1)} %get-tuple-element.27), channel_id=1, source_target_pairs={{0,2},{1,3},{2,0},{3,1},{4,6},{5,7},{6,4},{7,5},{8,10},{9,11},{10,... | collective-permute-start | bytes 49160 | tf_op jit(solution)/shard_map/ppermute | solution.py:204
  20.0 1.3 %collective-permute-start.9 = (f32[32,128]{1,0:T(8,128)S(1)}, f32[32,128]{1,0:T(8,128)S(1)}, u32[]{:S(2)}, u32[]{:S(2)}) collective-permute-start(f32[32,128]{1,0:T(8,128)S(1)} %get-tuple-element.28), channel_id=1, source_target_pairs={{0,1},{1,0},{2,3},{3,2},{4,5},{5,4},{6,7},{7,6},{8,9},{9,8},{10,11... | collective-permute-start | bytes 49160 | tf_op jit(solution)/shard_map/ppermute | solution.py:204
  21.4 1.2 %collective-permute-done.7.refs_1_ = f32[32,128]{1,0:T(8,128)S(1)} collective-permute-done((f32[32,128]{1,0:T(8,128)S(1)}, f32[32,128]{1,0:T(8,128)S(1)}, u32[]{:S(2)}, u32[]{:S(2)}) %collective-permute-start.7) | collective-permute-done | bytes 16416 | tf_op jit(solution)/shard_map/ppermute | solution.py:204
  22.6 1.5 %collective-permute-done.8.refs_2_ = f32[32,128]{1,0:T(8,128)S(1)} collective-permute-done((f32[32,128]{1,0:T(8,128)S(1)}, f32[32,128]{1,0:T(8,128)S(1)}, u32[]{:S(2)}, u32[]{:S(2)}) %collective-permute-start.8) | collective-permute-done | bytes 16416 | tf_op jit(solution)/shard_map/ppermute | solution.py:204
  24.1 0.0 collective-permute-done.9.refs_3_
  24.1 0.7 %sum_divide.1 = f32[32,64]{1,0:T(8,128)} custom-call(f32[32,128]{1,0:T(8,128)S(1)} %get-tuple-element.25.refs_0_, f32[32,128]{1,0:T(8,128)S(1)} %collective-permute-done.7.refs_1_, f32[32,128]{1,0:T(8,128)S(1)} %collective-permute-done.8.refs_2_, f32[32,128]{1,0:T(8,128)S(1)} %collective-permute-done.9.refs_3_), custom_call_target="tpu_custom_call" | custom-call | bytes 65536 | tf_op jit(solution)/shard_map/sum_divide/pallas_call | solution.py:210
  (2 shorter events, 0.0 us)
Async XLA Ops:
  0.0 10.1 %collective-permute-start = (f32[3,32,256]{2,1,0:T(8,128)}, f32[3,32,256]{2,1,0:T(8,128)S(1)}, u32[]{:S(2)}, u32[]{:S(2)}) collective-permute-start(f32[3,32,256]{2,1,0:T(8,128)} %refs_0_.1), channel_id=1, source_target_pairs={{0,2},{1,3},{2,0},{3,1},{4,6},{5,7},{6,4},{7,5},{8,10},{9,11},{10,... | collective-permute-start | bytes 294920 | tf_op jit(solution)/shard_map/ppermute | solution.py:204
  5.0 3.6 %copy-start = (f32[3,32,256]{2,1,0:T(8,128)S(1)}, f32[3,32,256]{2,1,0:T(8,128)}, u32[]{:S(2)}) copy-start(f32[3,32,256]{2,1,0:T(8,128)} %refs_0_.1) | copy-start | bytes 294916
  5.0 5.6 %collective-permute-start.3 = (f32[104,256]{1,0:T(8,128)S(1)}, f32[104,256]{1,0:T(8,128)S(1)}, u32[]{:S(2)}, u32[]{:S(2)}) collective-permute-start(f32[104,256]{1,0:T(8,128)S(1)} %pack.1.refs_0_), channel_id=1, source_target_pairs={{0,8},{4,12},{8,0},{12,4},{16,24},{20,28},{24,16},{28,20},{1,9},{5... | collective-permute-start | bytes 319496 | tf_op jit(solution)/shard_map/ppermute | solution.py:204
  6.5 5.8 %collective-permute-start.4 = (f32[104,256]{1,0:T(8,128)S(1)}, f32[104,256]{1,0:T(8,128)S(1)}, u32[]{:S(2)}, u32[]{:S(2)}) collective-permute-start(f32[104,256]{1,0:T(8,128)S(1)} %pack.1.refs_0_), channel_id=1, source_target_pairs={{0,16},{4,20},{8,24},{12,28},{16,0},{20,4},{24,8},{28,12},{1,17},{... | collective-permute-start | bytes 319496 | tf_op jit(solution)/shard_map/ppermute | solution.py:204
  8.1 5.6 %collective-permute-start.5 = (f32[104,256]{1,0:T(8,128)S(1)}, f32[104,256]{1,0:T(8,128)S(1)}, u32[]{:S(2)}, u32[]{:S(2)}) collective-permute-start(f32[104,256]{1,0:T(8,128)S(1)} %pack.1.refs_0_), channel_id=1, source_target_pairs={{0,24},{4,28},{8,16},{12,20},{16,8},{20,12},{24,0},{28,4},{1,25},{... | collective-permute-start | bytes 319496 | tf_op jit(solution)/shard_map/ppermute | solution.py:204
  8.6 5.2 %collective-permute-start.2 = (f32[3,32,256]{2,1,0:T(8,128)S(1)}, f32[3,32,256]{2,1,0:T(8,128)S(1)}, u32[]{:S(2)}, u32[]{:S(2)}) collective-permute-start(f32[3,32,256]{2,1,0:T(8,128)S(1)} %copy-done), channel_id=1, source_target_pairs={{0,1},{1,0},{2,3},{3,2},{4,5},{5,4},{6,7},{7,6},{8,9},{9,8},{10,11... | collective-permute-start | bytes 294920 | tf_op jit(solution)/shard_map/ppermute | solution.py:204
  10.1 4.7 %collective-permute-start.1 = (f32[3,32,256]{2,1,0:T(8,128)S(1)}, f32[3,32,256]{2,1,0:T(8,128)S(1)}, u32[]{:S(2)}, u32[]{:S(2)}) collective-permute-start(f32[3,32,256]{2,1,0:T(8,128)S(1)} %far_rows.1.refs_4_.refs_1_), channel_id=1, source_target_pairs={{0,1},{1,0},{2,3},{3,2},{4,5},{5,4},{6,7},{7,6},{8,9},{9,8},{10,11... | collective-permute-start | bytes 294920 | tf_op jit(solution)/shard_map/ppermute | solution.py:204
  13.7 1.8 %collective-permute-start.6 = (f32[4,104,256]{2,1,0:T(8,128)S(1)}, f32[4,104,256]{2,1,0:T(8,128)S(1)}, u32[]{:S(2)}, u32[]{:S(2)}) collective-permute-start(f32[4,104,256]{2,1,0:T(8,128)S(1)} %columns.1.refs_3_.own_ref), channel_id=1, source_target_pairs={{0,4},{4,0},{8,12},{12,8},{16,20},{20,16},{24,28},{28,24},{1,5},{5... | collective-permute-start | bytes 1277960 | tf_op jit(solution)/shard_map/ppermute | solution.py:204
  16.9 5.6 %collective-permute-start.7 = (f32[32,128]{1,0:T(8,128)S(1)}, f32[32,128]{1,0:T(8,128)S(1)}, u32[]{:S(2)}, u32[]{:S(2)}) collective-permute-start(f32[32,128]{1,0:T(8,128)S(1)} %get-tuple-element.26), channel_id=1, source_target_pairs={{0,3},{1,2},{2,1},{3,0},{4,7},{5,6},{6,5},{7,4},{8,11},{9,10},{10,... | collective-permute-start | bytes 49160 | tf_op jit(solution)/shard_map/ppermute | solution.py:204
  19.5 4.6 %collective-permute-start.8 = (f32[32,128]{1,0:T(8,128)S(1)}, f32[32,128]{1,0:T(8,128)S(1)}, u32[]{:S(2)}, u32[]{:S(2)}) collective-permute-start(f32[32,128]{1,0:T(8,128)S(1)} %get-tuple-element.27), channel_id=1, source_target_pairs={{0,2},{1,3},{2,0},{3,1},{4,6},{5,7},{6,4},{7,5},{8,10},{9,11},{10,... | collective-permute-start | bytes 49160 | tf_op jit(solution)/shard_map/ppermute | solution.py:204
  20.0 4.1 %collective-permute-start.9 = (f32[32,128]{1,0:T(8,128)S(1)}, f32[32,128]{1,0:T(8,128)S(1)}, u32[]{:S(2)}, u32[]{:S(2)}) collective-permute-start(f32[32,128]{1,0:T(8,128)S(1)} %get-tuple-element.28), channel_id=1, source_target_pairs={{0,1},{1,0},{2,3},{3,2},{4,5},{5,4},{6,7},{7,6},{8,9},{9,8},{10,11... | collective-permute-start | bytes 49160 | tf_op jit(solution)/shard_map/ppermute | solution.py:204

commit v5 on v4

--- a/solution.py
+++ b/solution.py
@@ -10,6 +10,7 @@
 NEWTON = 8
 BAND = 2.0
 LANES = 128
+CHUNK = 16
 VM = pl.BlockSpec(memory_space=pltpu.VMEM)
 NT = (((1,), (1,)), ((), ()))
 
@@ -138,13 +139,13 @@
     count_cols = norm.shape[1]
     atoms = side.shape[1] // 3
     moment[0:3 * count, :] = lax.dot_general(rows, side, NT, preferred_element_type=jnp.float32)
-    for at in range(0, count, 8):
+    for at in range(0, count, CHUNK):
         m = [
-            moment[a * count + at:a * count + at + 8, b * count_cols:(b + 1) * count_cols]
+            moment[a * count + at:a * count + at + CHUNK, b * count_cols:(b + 1) * count_cols]
             for a in range(3) for b in range(3)
         ]
-        half_norm = 0.5 * (row_norm[at:at + 8, 0:1] + norm[0:1, :])
-        tile[at:at + 8, :] = eigen_tile(m, half_norm, atoms)
+        half_norm = 0.5 * (row_norm[at:at + CHUNK, 0:1] + norm[0:1, :])
+        tile[at:at + CHUNK, :] = eigen_tile(m, half_norm, atoms)
 
 
 def early_kernel(n_early, *refs):

time: 25 us -> 25 us (level)
  no operation moved by 1% of the time
where the time goes in v5:
time: 25 us; the launch traced here: 24.8 us
  starting transfers between devices  14.2 us (57%)
  waiting for transfers between devices  5.86 us (23%)
  Pallas kernels  3.76 us (15%)
  other arithmetic  0.92 us (4%)
    ppermute x10, starting transfers between devices, exchange(): return lax.ppermute(x, axis, [(at, at ^ mask) for at in range(count)])  14.2 us
    ppermute x10, waiting for transfers between devices, exchange(): return lax.ppermute(x, axis, [(at, at ^ mask) for at in range(count)])  5.86 us
    pallas_call x7, Pallas kernels, call(): pl.pallas_call(kernel, out_shape=out_shape, in_specs=[VM] * len(ins), out...  3.76 us
    concatenate x1, other arithmetic, per_device(): jnp.concatenate([col_frames.reshape(comps * frames, atoms), jnp.pad(vecto...  0.92 us
  transfers between devices with their start and end apart: 10, of which 5 were waited for; matrix products, arithmetic and copies ran while one was open for 4% of the time, Pallas kernels for 7%

profile of v5, /device:TPU:0, one launch (start us, length us, event | category | flops | bytes accessed | tf_op | source)
XLA Modules:
  0.0 24.8 jit_solution(3715677560193930710)
XLA Ops:
  0.0 4.0 %collective-permute-start = (f32[3,32,256]{2,1,0:T(8,128)}, f32[3,32,256]{2,1,0:T(8,128)S(1)}, u32[]{:S(2)}, u32[]{:S(2)}) collective-permute-start(f32[3,32,256]{2,1,0:T(8,128)} %refs_0_.1), channel_id=1, source_target_pairs={{0,2},{1,3},{2,0},{3,1},{4,6},{5,7},{6,4},{7,5},{8,10},{9,11},{10,... | collective-permute-start | bytes 294920 | tf_op jit(solution)/shard_map/ppermute | solution.py:205
  4.0 0.9 %select_maximum_fusion.in_ref = f32[128,256]{1,0:T(8,128)S(1)} fusion(f32[32,64]{1,0:T(8,128)} %bitcast.4, f32[96,256]{1,0:T(8,128)} %bitcast.3), kind=kLoop, calls=%fused_computation | loop fusion | flops 98304 | bytes 237568 | tf_op jit(solution)/shard_map/concatenate | solution.py:232
  5.0 0.0 copy-start
  5.0 0.1 pack.1.refs_0_
  5.0 1.5 %collective-permute-start.3 = (f32[104,256]{1,0:T(8,128)S(1)}, f32[104,256]{1,0:T(8,128)S(1)}, u32[]{:S(2)}, u32[]{:S(2)}) collective-permute-start(f32[104,256]{1,0:T(8,128)S(1)} %pack.1.refs_0_), channel_id=1, source_target_pairs={{0,8},{4,12},{8,0},{12,4},{16,24},{20,28},{24,16},{28,20},{1,9},{5... | collective-permute-start | bytes 319496 | tf_op jit(solution)/shard_map/ppermute | solution.py:205
  6.5 1.5 %collective-permute-start.4 = (f32[104,256]{1,0:T(8,128)S(1)}, f32[104,256]{1,0:T(8,128)S(1)}, u32[]{:S(2)}, u32[]{:S(2)}) collective-permute-start(f32[104,256]{1,0:T(8,128)S(1)} %pack.1.refs_0_), channel_id=1, source_target_pairs={{0,16},{4,20},{8,24},{12,28},{16,0},{20,4},{24,8},{28,12},{1,17},{... | collective-permute-start | bytes 319496 | tf_op jit(solution)/shard_map/ppermute | solution.py:205
  8.1 0.5 %collective-permute-start.5 = (f32[104,256]{1,0:T(8,128)S(1)}, f32[104,256]{1,0:T(8,128)S(1)}, u32[]{:S(2)}, u32[]{:S(2)}) collective-permute-start(f32[104,256]{1,0:T(8,128)S(1)} %pack.1.refs_0_), channel_id=1, source_target_pairs={{0,24},{4,28},{8,16},{12,20},{16,8},{20,12},{24,0},{28,4},{1,25},{... | collective-permute-start | bytes 319496 | tf_op jit(solution)/shard_map/ppermute | solution.py:205
  8.5 0.0 copy-done
  8.6 1.6 %collective-permute-start.2 = (f32[3,32,256]{2,1,0:T(8,128)S(1)}, f32[3,32,256]{2,1,0:T(8,128)S(1)}, u32[]{:S(2)}, u32[]{:S(2)}) collective-permute-start(f32[3,32,256]{2,1,0:T(8,128)S(1)} %copy-done), channel_id=1, source_target_pairs={{0,1},{1,0},{2,3},{3,2},{4,5},{5,4},{6,7},{7,6},{8,9},{9,8},{10,11... | collective-permute-start | bytes 294920 | tf_op jit(solution)/shard_map/ppermute | solution.py:205
  10.1 0.0 collective-permute-done.in_ref
  10.1 0.5 %collective-permute-start.1 = (f32[3,32,256]{2,1,0:T(8,128)S(1)}, f32[3,32,256]{2,1,0:T(8,128)S(1)}, u32[]{:S(2)}, u32[]{:S(2)}) collective-permute-start(f32[3,32,256]{2,1,0:T(8,128)S(1)} %far_rows.1.refs_4_.refs_1_), channel_id=1, source_target_pairs={{0,1},{1,0},{2,3},{3,2},{4,5},{5,4},{6,7},{7,6},{8,9},{9,8},{10,11... | collective-permute-start | bytes 294920 | tf_op jit(solution)/shard_map/ppermute | solution.py:205
  10.7 0.0 collective-permute-done.3.refs_1_
  10.7 1.7 %collective-permute-done.4.refs_2_ = f32[104,256]{1,0:T(8,128)S(1)} collective-permute-done((f32[104,256]{1,0:T(8,128)S(1)}, f32[104,256]{1,0:T(8,128)S(1)}, u32[]{:S(2)}, u32[]{:S(2)}) %collective-permute-start.4) | collective-permute-done | bytes 106528 | tf_op jit(solution)/shard_map/ppermute | solution.py:205
  12.4 1.3 %collective-permute-done.5.refs_3_ = f32[104,256]{1,0:T(8,128)S(1)} collective-permute-done((f32[104,256]{1,0:T(8,128)S(1)}, f32[104,256]{1,0:T(8,128)S(1)}, u32[]{:S(2)}, u32[]{:S(2)}) %collective-permute-start.5) | collective-permute-done | bytes 106528 | tf_op jit(solution)/shard_map/ppermute | solution.py:205
  13.7 0.1 collective-permute-start.6
  13.8 0.0 collective-permute-done.2.refs_2_
  13.8 1.1 %early_tile.1 = (bf16[1,384,768]{2,1,0:T(8,128)(2,1)S(1)}, f32[1,128,128]{2,1,0:T(8,128)S(1)}, f32[1,128,128]{2,1,0:T(8,128)S(1)}, bf16[384,768]{1,0:T(8,128)(2,1)S(1)}, f32[8,128]{1,0:T(8,128)S(1)}) custom-call(f32[3,32,256]{2,1,0:T(8,128)S(1)} %copy-done, f32[3,32,256]{2,1,0:T(8,128)S(1)} %far_rows.1.refs_4_.refs_1_, ...), custom_call_target="tpu_custom_call" | custom-call | flops 226492416 | bytes 720896 | tf_op jit(solution)/shard_map/early_tile/pallas_call | solution.py:211
  14.9 0.0 collective-permute-done.1.row_ref
  14.9 0.5 %last_tile.1 = (bf16[1,384,768]{2,1,0:T(8,128)(2,1)S(1)}, f32[1,128,128]{2,1,0:T(8,128)S(1)}, f32[1,128,128]{2,1,0:T(8,128)S(1)}) custom-call(f32[3,32,256]{2,1,0:T(8,128)S(1)} %collective-permute-done.1.row_ref, bf16[384,768]{1,0:T(8,128)(2,1)S(1)} %get-tuple-element.17.side_ref, ...), custom_call_target="tpu_custom_call", output_to_operand_aliasing={{0}: (3, {}), {1}: (4, {}), {2}: (5, {})} | custom-call | flops 57982058496 | bytes 2592768 | tf_op jit(solution)/shard_map/last_tile/pallas_call | solution.py:211
  15.4 0.1 collective-permute-done.6.blocks_ref
  15.5 1.4 %second_tile.1 = (f32[32,128]{1,0:T(8,128)S(1)}, f32[32,128]{1,0:T(8,128)S(1)}, f32[32,128]{1,0:T(8,128)S(1)}, f32[32,128]{1,0:T(8,128)S(1)}) custom-call(bf16[1,384,768]{2,1,0:T(8,128)(2,1)S(1)} %get-tuple-element.22.rows_ref, f32[1,128,128]{2,1,0:T(8,128)S(1)} %get-tuple-element.23.row_norm_ref, f32[1,128,128]{2,1,0:T(8,128)S(1)} %get-tuple-element.24.tile_ref, ...), custom_call_target="tpu_custom_call" | custom-call | flops 226492416 | bytes 2162688 | tf_op jit(solution)/shard_map/second_tile/pallas_call | solution.py:211
  16.9 2.5 %collective-permute-start.7 = (f32[32,128]{1,0:T(8,128)S(1)}, f32[32,128]{1,0:T(8,128)S(1)}, u32[]{:S(2)}, u32[]{:S(2)}) collective-permute-start(f32[32,128]{1,0:T(8,128)S(1)} %get-tuple-element.26), channel_id=1, source_target_pairs={{0,3},{1,2},{2,1},{3,0},{4,7},{5,6},{6,5},{7,4},{8,11},{9,10},{10,... | collective-permute-start | bytes 49160 | tf_op jit(solution)/shard_map/ppermute | solution.py:205
  19.5 0.6 %collective-permute-start.8 = (f32[32,128]{1,0:T(8,128)S(1)}, f32[32,128]{1,0:T(8,128)S(1)}, u32[]{:S(2)}, u32[]{:S(2)}) collective-permute-start(f32[32,128]{1,0:T(8,128)S(1)} %get-tuple-element.27), channel_id=1, source_target_pairs={{0,2},{1,3},{2,0},{3,1},{4,6},{5,7},{6,4},{7,5},{8,10},{9,11},{10,... | collective-permute-start | bytes 49160 | tf_op jit(solution)/shard_map/ppermute | solution.py:205
  20.0 1.3 %collective-permute-start.9 = (f32[32,128]{1,0:T(8,128)S(1)}, f32[32,128]{1,0:T(8,128)S(1)}, u32[]{:S(2)}, u32[]{:S(2)}) collective-permute-start(f32[32,128]{1,0:T(8,128)S(1)} %get-tuple-element.28), channel_id=1, source_target_pairs={{0,1},{1,0},{2,3},{3,2},{4,5},{5,4},{6,7},{7,6},{8,9},{9,8},{10,11... | collective-permute-start | bytes 49160 | tf_op jit(solution)/shard_map/ppermute | solution.py:205
  21.4 1.2 %collective-permute-done.7.refs_1_ = f32[32,128]{1,0:T(8,128)S(1)} collective-permute-done((f32[32,128]{1,0:T(8,128)S(1)}, f32[32,128]{1,0:T(8,128)S(1)}, u32[]{:S(2)}, u32[]{:S(2)}) %collective-permute-start.7) | collective-permute-done | bytes 16416 | tf_op jit(solution)/shard_map/ppermute | solution.py:205
  22.5 1.5 %collective-permute-done.8.refs_2_ = f32[32,128]{1,0:T(8,128)S(1)} collective-permute-done((f32[32,128]{1,0:T(8,128)S(1)}, f32[32,128]{1,0:T(8,128)S(1)}, u32[]{:S(2)}, u32[]{:S(2)}) %collective-permute-start.8) | collective-permute-done | bytes 16416 | tf_op jit(solution)/shard_map/ppermute | solution.py:205
  24.1 0.0 collective-permute-done.9.refs_3_
  24.1 0.7 %sum_divide.1 = f32[32,64]{1,0:T(8,128)} custom-call(f32[32,128]{1,0:T(8,128)S(1)} %get-tuple-element.25.refs_0_, f32[32,128]{1,0:T(8,128)S(1)} %collective-permute-done.7.refs_1_, f32[32,128]{1,0:T(8,128)S(1)} %collective-permute-done.8.refs_2_, f32[32,128]{1,0:T(8,128)S(1)} %collective-permute-done.9.refs_3_), custom_call_target="tpu_custom_call" | custom-call | bytes 65536 | tf_op jit(solution)/shard_map/sum_divide/pallas_call | solution.py:211
  (2 shorter events, 0.0 us)
Async XLA Ops:
  0.0 10.1 %collective-permute-start = (f32[3,32,256]{2,1,0:T(8,128)}, f32[3,32,256]{2,1,0:T(8,128)S(1)}, u32[]{:S(2)}, u32[]{:S(2)}) collective-permute-start(f32[3,32,256]{2,1,0:T(8,128)} %refs_0_.1), channel_id=1, source_target_pairs={{0,2},{1,3},{2,0},{3,1},{4,6},{5,7},{6,4},{7,5},{8,10},{9,11},{10,... | collective-permute-start | bytes 294920 | tf_op jit(solution)/shard_map/ppermute | solution.py:205
  5.0 3.6 %copy-start = (f32[3,32,256]{2,1,0:T(8,128)S(1)}, f32[3,32,256]{2,1,0:T(8,128)}, u32[]{:S(2)}) copy-start(f32[3,32,256]{2,1,0:T(8,128)} %refs_0_.1) | copy-start | bytes 294916
  5.0 5.6 %collective-permute-start.3 = (f32[104,256]{1,0:T(8,128)S(1)}, f32[104,256]{1,0:T(8,128)S(1)}, u32[]{:S(2)}, u32[]{:S(2)}) collective-permute-start(f32[104,256]{1,0:T(8,128)S(1)} %pack.1.refs_0_), channel_id=1, source_target_pairs={{0,8},{4,12},{8,0},{12,4},{16,24},{20,28},{24,16},{28,20},{1,9},{5... | collective-permute-start | bytes 319496 | tf_op jit(solution)/shard_map/ppermute | solution.py:205
  6.5 5.8 %collective-permute-start.4 = (f32[104,256]{1,0:T(8,128)S(1)}, f32[104,256]{1,0:T(8,128)S(1)}, u32[]{:S(2)}, u32[]{:S(2)}) collective-permute-start(f32[104,256]{1,0:T(8,128)S(1)} %pack.1.refs_0_), channel_id=1, source_target_pairs={{0,16},{4,20},{8,24},{12,28},{16,0},{20,4},{24,8},{28,12},{1,17},{... | collective-permute-start | bytes 319496 | tf_op jit(solution)/shard_map/ppermute | solution.py:205
  8.1 5.6 %collective-permute-start.5 = (f32[104,256]{1,0:T(8,128)S(1)}, f32[104,256]{1,0:T(8,128)S(1)}, u32[]{:S(2)}, u32[]{:S(2)}) collective-permute-start(f32[104,256]{1,0:T(8,128)S(1)} %pack.1.refs_0_), channel_id=1, source_target_pairs={{0,24},{4,28},{8,16},{12,20},{16,8},{20,12},{24,0},{28,4},{1,25},{... | collective-permute-start | bytes 319496 | tf_op jit(solution)/shard_map/ppermute | solution.py:205
  8.6 5.2 %collective-permute-start.2 = (f32[3,32,256]{2,1,0:T(8,128)S(1)}, f32[3,32,256]{2,1,0:T(8,128)S(1)}, u32[]{:S(2)}, u32[]{:S(2)}) collective-permute-start(f32[3,32,256]{2,1,0:T(8,128)S(1)} %copy-done), channel_id=1, source_target_pairs={{0,1},{1,0},{2,3},{3,2},{4,5},{5,4},{6,7},{7,6},{8,9},{9,8},{10,11... | collective-permute-start | bytes 294920 | tf_op jit(solution)/shard_map/ppermute | solution.py:205
  10.1 4.7 %collective-permute-start.1 = (f32[3,32,256]{2,1,0:T(8,128)S(1)}, f32[3,32,256]{2,1,0:T(8,128)S(1)}, u32[]{:S(2)}, u32[]{:S(2)}) collective-permute-start(f32[3,32,256]{2,1,0:T(8,128)S(1)} %far_rows.1.refs_4_.refs_1_), channel_id=1, source_target_pairs={{0,1},{1,0},{2,3},{3,2},{4,5},{5,4},{6,7},{7,6},{8,9},{9,8},{10,11... | collective-permute-start | bytes 294920 | tf_op jit(solution)/shard_map/ppermute | solution.py:205
  13.7 1.8 %collective-permute-start.6 = (f32[4,104,256]{2,1,0:T(8,128)S(1)}, f32[4,104,256]{2,1,0:T(8,128)S(1)}, u32[]{:S(2)}, u32[]{:S(2)}) collective-permute-start(f32[4,104,256]{2,1,0:T(8,128)S(1)} %columns.1.refs_3_.own_ref), channel_id=1, source_target_pairs={{0,4},{4,0},{8,12},{12,8},{16,20},{20,16},{24,28},{28,24},{1,5},{5... | collective-permute-start | bytes 1277960 | tf_op jit(solution)/shard_map/ppermute | solution.py:205
  16.9 5.6 %collective-permute-start.7 = (f32[32,128]{1,0:T(8,128)S(1)}, f32[32,128]{1,0:T(8,128)S(1)}, u32[]{:S(2)}, u32[]{:S(2)}) collective-permute-start(f32[32,128]{1,0:T(8,128)S(1)} %get-tuple-element.26), channel_id=1, source_target_pairs={{0,3},{1,2},{2,1},{3,0},{4,7},{5,6},{6,5},{7,4},{8,11},{9,10},{10,... | collective-permute-start | bytes 49160 | tf_op jit(solution)/shard_map/ppermute | solution.py:205
  19.5 4.6 %collective-permute-start.8 = (f32[32,128]{1,0:T(8,128)S(1)}, f32[32,128]{1,0:T(8,128)S(1)}, u32[]{:S(2)}, u32[]{:S(2)}) collective-permute-start(f32[32,128]{1,0:T(8,128)S(1)} %get-tuple-element.27), channel_id=1, source_target_pairs={{0,2},{1,3},{2,0},{3,1},{4,6},{5,7},{6,4},{7,5},{8,10},{9,11},{10,... | collective-permute-start | bytes 49160 | tf_op jit(solution)/shard_map/ppermute | solution.py:205
  20.0 4.1 %collective-permute-start.9 = (f32[32,128]{1,0:T(8,128)S(1)}, f32[32,128]{1,0:T(8,128)S(1)}, u32[]{:S(2)}, u32[]{:S(2)}) collective-permute-start(f32[32,128]{1,0:T(8,128)S(1)} %get-tuple-element.28), channel_id=1, source_target_pairs={{0,1},{1,0},{2,3},{3,2},{4,5},{5,4},{6,7},{7,6},{8,9},{9,8},{10,11... | collective-permute-start | bytes 49160 | tf_op jit(solution)/shard_map/ppermute | solution.py:205
